TPU v7x, 32 devices: a whole 2x2x4 slice. The times are simulated.
32 devices in a mesh: dp: 16 (over z, x, core), seq: 2 (over y).
Axes of the slice: x: 2, y: 2, z: 4, core: 2. Of those that a mesh axis runs over, the one named last changes fastest.
Arguments:
- hidden_in: bfloat16 [32, 1024, 768], P('dp', 'seq'), may hold values from -6 to 6
- memory: bfloat16 [32, 1024, 768], P('dp', 'seq'), may hold values from -6 to 6
- tgt_segment: int32 [32, 1024], P('dp', 'seq'), may hold values from 0 to 3, as said below
- src_segment: int32 [32, 1024], P('dp', 'seq'), may hold values from 0 to 3, as said below
- out_grad: bfloat16 [32, 1024, 768], P('dp', 'seq'), may hold values from -6 to 6
- self_query: bfloat16 [768, 768], replicated, may hold values from -0.21875 to 0.21875
- query_bias: bfloat16 [768], replicated, may hold values from -1.75 to 1.75
- self_key: bfloat16 [768, 768], replicated, may hold values from -0.21875 to 0.21875
- self_value: bfloat16 [768, 768], replicated, may hold values from -0.21875 to 0.21875
- value_bias: bfloat16 [768], replicated, may hold values from -0.3125 to 0.3125
- self_output: bfloat16 [768, 768], replicated, may hold values from -1.25 to 1.25
- output_bias: bfloat16 [768], replicated, may hold values from -1.75 to 1.75
- first_gain: bfloat16 [768], replicated, may hold values from 0.5 to 1.5
- first_shift: bfloat16 [768], replicated, may hold values from -1.75 to 1.75
- cross_query: bfloat16 [768, 768], replicated, may hold values from -0.21875 to 0.21875
- cross_query_bias: bfloat16 [768], replicated, may hold values from -1.75 to 1.75
- cross_key: bfloat16 [768, 768], replicated, may hold values from -0.21875 to 0.21875
- cross_value: bfloat16 [768, 768], replicated, may hold values from -0.21875 to 0.21875
- cross_value_bias: bfloat16 [768], replicated, may hold values from -0.3125 to 0.3125
- cross_output: bfloat16 [768, 768], replicated, may hold values from -1.25 to 1.25
- cross_output_bias: bfloat16 [768], replicated, may hold values from -1.75 to 1.75
- second_gain: bfloat16 [768], replicated, may hold values from 0.5 to 1.5
- second_shift: bfloat16 [768], replicated, may hold values from -1.75 to 1.75
- ffn_in: bfloat16 [768, 3072], replicated, may hold values from -0.21875 to 0.21875
- ffn_in_bias: bfloat16 [3072], replicated, may hold values from -3 to 3
- ffn_out: bfloat16 [3072, 768], replicated, may hold values from -0.109375 to 0.109375
- ffn_out_bias: bfloat16 [768], replicated, may hold values from -1.75 to 1.75
- third_gain: bfloat16 [768], replicated, may hold values from 0.5 to 1.5
- third_shift: bfloat16 [768], replicated, may hold values from -1.75 to 1.75
Outputs:
- hidden_out: bfloat16 [32, 1024, 768], P('dp', 'seq')
- hidden_grad: bfloat16 [32, 1024, 768], P('dp', 'seq')
- memory_grad: bfloat16 [32, 1024, 768], P('dp', 'seq')
- grad_self_query: float32 [768, 768], P('dp')
- grad_query_bias: float32 [768], P('dp')
- grad_self_key: float32 [768, 768], P('dp')
- grad_self_value: float32 [768, 768], P('dp')
- grad_value_bias: float32 [768], P('dp')
- grad_self_output: float32 [768, 768], P('dp')
- grad_output_bias: float32 [768], P('dp')
- grad_first_gain: float32 [768], P('dp')
- grad_first_shift: float32 [768], P('dp')
- grad_cross_query: float32 [768, 768], P('dp')
- grad_cross_query_bias: float32 [768], P('dp')
- grad_cross_key: float32 [768, 768], P('dp')
- grad_cross_value: float32 [768, 768], P('dp')
- grad_cross_value_bias: float32 [768], P('dp')
- grad_cross_output: float32 [768, 768], P('dp')
- grad_cross_output_bias: float32 [768], P('dp')
- grad_second_gain: float32 [768], P('dp')
- grad_second_shift: float32 [768], P('dp')
- grad_ffn_in: float32 [768, 3072], P('dp')
- grad_ffn_in_bias: float32 [3072], P('dp')
- grad_ffn_out: float32 [3072, 768], P('dp')
- grad_ffn_out_bias: float32 [768], P('dp')
- grad_third_gain: float32 [768], P('dp')
- grad_third_shift: float32 [768], P('dp')
Inputs may be any that keep to these rules, and one draw needn't show every extreme that they name: `tgt_segment`: in every row the ids 0, 1, 2, 3 each occur and never fall; documents 0 and 1 end before position 512, document 3 starts after position 512. `src_segment`: in every row the ids 0, 1, 2, 3 each occur and never fall; documents 0 and 1 end before position 512, document 3 starts after position 512.
All inputs are finite; a program needn't handle non-finite values.
Results may differ from a plain program's by a relative error of at most 0.025.
Values may be sent and summed in bfloat16 or wider, within the bound.
No kernel may reach another device: no remote copies, remote signals or barrier semaphores. Data moves between devices by JAX's collectives and lax.ppermute only.
A program may use at most 448 MiB of HBM per device.

v0:
```python
import math

import jax
import jax.numpy as jnp
from jax import lax
from jax.sharding import PartitionSpec as P

HEADS = 12


def project(values, weight):
    return jnp.dot(values, weight, preferred_element_type=jnp.float32)


def project_back(gradient, weight):
    return jnp.einsum("rte,de->rtd", gradient, weight, preferred_element_type=jnp.float32)


def weight_grad(values, gradient):
    return jnp.einsum("rtd,rte->de", values, gradient, preferred_element_type=jnp.float32)


def token_sum(gradient):
    return jnp.sum(gradient.astype(jnp.float32), axis=(0, 1))


def layer_norm(values, norm_gain, norm_shift):
    center = values - jnp.mean(values, axis=-1, keepdims=True)
    spread = jnp.mean(center * center, axis=-1, keepdims=True)
    return center * lax.rsqrt(spread + 1e-05) * norm_gain + norm_shift


def exact_gelu(values):
    return jax.nn.gelu(values, approximate=False)


def split_heads(values):
    return values.reshape(values.shape[0], values.shape[1], HEADS, values.shape[2] // HEADS)


def merge_heads(values):
    return values.reshape(values.shape[0], values.shape[1], values.shape[2] * values.shape[3])


def masked_scores(queries, key_rows, allowed):
    raw_scores = jnp.einsum(
        "rqhd,rkhd->rhqk",
        split_heads(queries),
        split_heads(key_rows),
        preferred_element_type=jnp.float32,
    )
    factor = 1.0 / math.sqrt(queries.shape[2] // HEADS)
    return jnp.where(allowed[:, None], raw_scores * factor, -1e30)


def attend_forward(queries, key_rows, value_rows, allowed):
    scores = masked_scores(queries, key_rows, allowed)
    highest = jnp.max(scores, axis=-1, keepdims=True)
    powers = jnp.exp(scores - highest)
    totals = jnp.sum(powers, axis=-1, keepdims=True)
    weights = (powers / totals).astype(jnp.bfloat16)
    mixed_heads = jnp.einsum(
        "rhqk,rkhd->rqhd", weights, split_heads(value_rows), preferred_element_type=jnp.float32
    )
    return (merge_heads(mixed_heads).astype(jnp.bfloat16), highest + jnp.log(totals))


def attend_backward(queries, key_rows, value_rows, allowed, log_totals, mixed_grad):
    scores = masked_scores(queries, key_rows, allowed)
    weights = jnp.exp(scores - log_totals)
    grad_heads = split_heads(mixed_grad)
    value_terms = jnp.einsum(
        "rhqk,rqhd->rkhd",
        weights.astype(jnp.bfloat16),
        grad_heads,
        preferred_element_type=jnp.float32,
    )
    weight_grads = jnp.einsum(
        "rqhd,rkhd->rhqk", grad_heads, split_heads(value_rows), preferred_element_type=jnp.float32
    )
    inner_sum = jnp.sum(weights * weight_grads, axis=-1, keepdims=True)
    factor = 1.0 / math.sqrt(queries.shape[2] // HEADS)
    score_grads = (weights * (weight_grads - inner_sum) * factor).astype(jnp.bfloat16)
    query_grads = jnp.einsum(
        "rhqk,rkhd->rqhd", score_grads, split_heads(key_rows), preferred_element_type=jnp.float32
    )
    key_terms = jnp.einsum(
        "rhqk,rqhd->rkhd", score_grads, split_heads(queries), preferred_element_type=jnp.float32
    )
    return (merge_heads(query_grads), merge_heads(key_terms), merge_heads(value_terms))


def on_device(
    hidden_in,
    memory,
    tgt_segment,
    src_segment,
    out_grad,
    self_query,
    query_bias,
    self_key,
    self_value,
    value_bias,
    self_output,
    output_bias,
    first_gain,
    first_shift,
    cross_query,
    cross_query_bias,
    cross_key,
    cross_value,
    cross_value_bias,
    cross_output,
    cross_output_bias,
    second_gain,
    second_shift,
    ffn_in,
    ffn_in_bias,
    ffn_out,
    ffn_out_bias,
    third_gain,
    third_shift,
):
    tokens = hidden_in.shape[1]
    queries = (project(hidden_in, self_query) + query_bias.astype(jnp.float32)).astype(jnp.bfloat16)
    key_rows = project(hidden_in, self_key).astype(jnp.bfloat16)
    value_rows = (project(hidden_in, self_value) + value_bias.astype(jnp.float32)).astype(
        jnp.bfloat16
    )
    target_ids = tgt_segment.astype(jnp.bfloat16)
    all_keys, all_values, all_target = (
        lax.all_gather(key_rows, "seq", axis=1, tiled=True),
        lax.all_gather(value_rows, "seq", axis=1, tiled=True),
        lax.all_gather(target_ids, "seq", axis=1, tiled=True),
    )
    memory_keys = project(memory, cross_key).astype(jnp.bfloat16)
    memory_values = (project(memory, cross_value) + cross_value_bias.astype(jnp.float32)).astype(
        jnp.bfloat16
    )
    all_memkeys, all_memvalues, all_source = (
        lax.all_gather(memory_keys, "seq", axis=1, tiled=True),
        lax.all_gather(memory_values, "seq", axis=1, tiled=True),
        lax.all_gather(src_segment.astype(jnp.bfloat16), "seq", axis=1, tiled=True),
    )
    offset = lax.axis_index("seq") * tokens
    query_places = offset + jnp.arange(tokens, dtype=jnp.int32)
    key_places = jnp.arange(all_keys.shape[1], dtype=jnp.int32)
    self_allowed = (target_ids[:, :, None] == all_target[:, None, :]) & (
        query_places[:, None] >= key_places[None, :]
    )[None]
    cross_allowed = target_ids[:, :, None] == all_source[:, None, :]
    self_mixed, self_totals = attend_forward(queries, all_keys, all_values, self_allowed)
    self_branch = project(self_mixed, self_output) + output_bias.astype(jnp.float32)
    first_norm, first_pull = jax.vjp(
        layer_norm,
        hidden_in.astype(jnp.float32) + self_branch,
        first_gain.astype(jnp.float32),
        first_shift.astype(jnp.float32),
    )
    first_low = first_norm.astype(jnp.bfloat16)
    cross_queries = (project(first_low, cross_query) + cross_query_bias.astype(jnp.float32)).astype(
        jnp.bfloat16
    )
    cross_mixed, cross_totals = attend_forward(
        cross_queries, all_memkeys, all_memvalues, cross_allowed
    )
    cross_branch = project(cross_mixed, cross_output) + cross_output_bias.astype(jnp.float32)
    second_norm, second_pull = jax.vjp(
        layer_norm,
        first_norm + cross_branch,
        second_gain.astype(jnp.float32),
        second_shift.astype(jnp.float32),
    )
    second_low = second_norm.astype(jnp.bfloat16)
    inner_rows = project(second_low, ffn_in) + ffn_in_bias.astype(jnp.float32)
    activation_full, gelu_pull = jax.vjp(exact_gelu, inner_rows)
    activation = activation_full.astype(jnp.bfloat16)
    ffn_branch = project(activation, ffn_out) + ffn_out_bias.astype(jnp.float32)
    final_norm, third_pull = jax.vjp(
        layer_norm,
        second_norm + ffn_branch,
        third_gain.astype(jnp.float32),
        third_shift.astype(jnp.float32),
    )
    hidden_out = final_norm.astype(jnp.bfloat16)
    third_back, grad_third_gain, grad_third_shift = third_pull(out_grad.astype(jnp.float32))
    ffn_back = third_back.astype(jnp.bfloat16)
    grad_ffn_out = weight_grad(activation, ffn_back)
    grad_ffn_out_bias = token_sum(ffn_back)
    activation_back = project_back(ffn_back, ffn_out)
    inner_back = gelu_pull(activation_back)[0].astype(jnp.bfloat16)
    grad_ffn_in = weight_grad(second_low, inner_back)
    grad_ffn_in_bias = token_sum(inner_back)
    second_back, grad_second_gain, grad_second_shift = second_pull(
        third_back + project_back(inner_back, ffn_in)
    )
    cross_back = second_back.astype(jnp.bfloat16)
    grad_cross_output = weight_grad(cross_mixed, cross_back)
    grad_cross_output_bias = token_sum(cross_back)
    cross_mixed_back = project_back(cross_back, cross_output).astype(jnp.bfloat16)
    cross_query_grad, memkey_terms, memvalue_terms = attend_backward(
        cross_queries, all_memkeys, all_memvalues, cross_allowed, cross_totals, cross_mixed_back
    )
    memkey_sum, memvalue_sum = (
        lax.psum_scatter(
            memkey_terms.astype(jnp.bfloat16), "seq", scatter_dimension=1, tiled=True
        ).astype(jnp.float32),
        lax.psum_scatter(
            memvalue_terms.astype(jnp.bfloat16), "seq", scatter_dimension=1, tiled=True
        ).astype(jnp.float32),
    )
    memory_key_back = memkey_sum.astype(jnp.bfloat16)
    memory_value_back = memvalue_sum.astype(jnp.bfloat16)
    cross_query_back = cross_query_grad.astype(jnp.bfloat16)
    grad_cross_query = weight_grad(first_low, cross_query_back)
    grad_cross_query_bias = token_sum(cross_query_back)
    grad_cross_key = weight_grad(memory, memory_key_back)
    grad_cross_value = weight_grad(memory, memory_value_back)
    grad_cross_value_bias = token_sum(memory_value_back)
    memory_grad = (
        project_back(memory_key_back, cross_key) + project_back(memory_value_back, cross_value)
    ).astype(jnp.bfloat16)
    first_back, grad_first_gain, grad_first_shift = first_pull(
        second_back + project_back(cross_query_back, cross_query)
    )
    self_back = first_back.astype(jnp.bfloat16)
    grad_self_output = weight_grad(self_mixed, self_back)
    grad_output_bias = token_sum(self_back)
    self_mixed_back = project_back(self_back, self_output).astype(jnp.bfloat16)
    query_grad, key_terms, value_terms = attend_backward(
        queries, all_keys, all_values, self_allowed, self_totals, self_mixed_back
    )
    key_sum, value_sum = (
        lax.psum_scatter(
            key_terms.astype(jnp.bfloat16), "seq", scatter_dimension=1, tiled=True
        ).astype(jnp.float32),
        lax.psum_scatter(
            value_terms.astype(jnp.bfloat16), "seq", scatter_dimension=1, tiled=True
        ).astype(jnp.float32),
    )
    key_back = key_sum.astype(jnp.bfloat16)
    value_back = value_sum.astype(jnp.bfloat16)
    query_back = query_grad.astype(jnp.bfloat16)
    grad_self_query = weight_grad(hidden_in, query_back)
    grad_query_bias = token_sum(query_back)
    grad_self_key = weight_grad(hidden_in, key_back)
    grad_self_value = weight_grad(hidden_in, value_back)
    grad_value_bias = token_sum(value_back)
    hidden_grad = (
        first_back
        + project_back(query_back, self_query)
        + project_back(key_back, self_key)
        + project_back(value_back, self_value)
    ).astype(jnp.bfloat16)
    partial_grads = [
        grad_self_query,
        grad_query_bias,
        grad_self_key,
        grad_self_value,
        grad_value_bias,
        grad_self_output,
        grad_output_bias,
        grad_first_gain,
        grad_first_shift,
        grad_cross_query,
        grad_cross_query_bias,
        grad_cross_key,
        grad_cross_value,
        grad_cross_value_bias,
        grad_cross_output,
        grad_cross_output_bias,
        grad_second_gain,
        grad_second_shift,
        grad_ffn_in,
        grad_ffn_in_bias,
        grad_ffn_out,
        grad_ffn_out_bias,
        grad_third_gain,
        grad_third_shift,
    ]
    summed = (
        lax.psum_scatter(
            partial_grads[0].astype(jnp.bfloat16), "dp", scatter_dimension=0, tiled=True
        ).astype(jnp.float32),
        lax.psum_scatter(
            partial_grads[1].astype(jnp.bfloat16), "dp", scatter_dimension=0, tiled=True
        ).astype(jnp.float32),
        lax.psum_scatter(
            partial_grads[2].astype(jnp.bfloat16), "dp", scatter_dimension=0, tiled=True
        ).astype(jnp.float32),
        lax.psum_scatter(
            partial_grads[3].astype(jnp.bfloat16), "dp", scatter_dimension=0, tiled=True
        ).astype(jnp.float32),
        lax.psum_scatter(
            partial_grads[4].astype(jnp.bfloat16), "dp", scatter_dimension=0, tiled=True
        ).astype(jnp.float32),
        lax.psum_scatter(
            partial_grads[5].astype(jnp.bfloat16), "dp", scatter_dimension=0, tiled=True
        ).astype(jnp.float32),
        lax.psum_scatter(
            partial_grads[6].astype(jnp.bfloat16), "dp", scatter_dimension=0, tiled=True
        ).astype(jnp.float32),
        lax.psum_scatter(
            partial_grads[7].astype(jnp.bfloat16), "dp", scatter_dimension=0, tiled=True
        ).astype(jnp.float32),
        lax.psum_scatter(
            partial_grads[8].astype(jnp.bfloat16), "dp", scatter_dimension=0, tiled=True
        ).astype(jnp.float32),
        lax.psum_scatter(
            partial_grads[9].astype(jnp.bfloat16), "dp", scatter_dimension=0, tiled=True
        ).astype(jnp.float32),
        lax.psum_scatter(
            partial_grads[10].astype(jnp.bfloat16), "dp", scatter_dimension=0, tiled=True
        ).astype(jnp.float32),
        lax.psum_scatter(
            partial_grads[11].astype(jnp.bfloat16), "dp", scatter_dimension=0, tiled=True
        ).astype(jnp.float32),
        lax.psum_scatter(
            partial_grads[12].astype(jnp.bfloat16), "dp", scatter_dimension=0, tiled=True
        ).astype(jnp.float32),
        lax.psum_scatter(
            partial_grads[13].astype(jnp.bfloat16), "dp", scatter_dimension=0, tiled=True
        ).astype(jnp.float32),
        lax.psum_scatter(
            partial_grads[14].astype(jnp.bfloat16), "dp", scatter_dimension=0, tiled=True
        ).astype(jnp.float32),
        lax.psum_scatter(
            partial_grads[15].astype(jnp.bfloat16), "dp", scatter_dimension=0, tiled=True
        ).astype(jnp.float32),
        lax.psum_scatter(
            partial_grads[16].astype(jnp.bfloat16), "dp", scatter_dimension=0, tiled=True
        ).astype(jnp.float32),
        lax.psum_scatter(
            partial_grads[17].astype(jnp.bfloat16), "dp", scatter_dimension=0, tiled=True
        ).astype(jnp.float32),
        lax.psum_scatter(
            partial_grads[18].astype(jnp.bfloat16), "dp", scatter_dimension=0, tiled=True
        ).astype(jnp.float32),
        lax.psum_scatter(
            partial_grads[19].astype(jnp.bfloat16), "dp", scatter_dimension=0, tiled=True
        ).astype(jnp.float32),
        lax.psum_scatter(
            partial_grads[20].astype(jnp.bfloat16), "dp", scatter_dimension=0, tiled=True
        ).astype(jnp.float32),
        lax.psum_scatter(
            partial_grads[21].astype(jnp.bfloat16), "dp", scatter_dimension=0, tiled=True
        ).astype(jnp.float32),
        lax.psum_scatter(
            partial_grads[22].astype(jnp.bfloat16), "dp", scatter_dimension=0, tiled=True
        ).astype(jnp.float32),
        lax.psum_scatter(
            partial_grads[23].astype(jnp.bfloat16), "dp", scatter_dimension=0, tiled=True
        ).astype(jnp.float32),
    )
    finished = (
        lax.psum(summed[0].astype(jnp.bfloat16), "seq").astype(jnp.float32),
        lax.psum(summed[1].astype(jnp.bfloat16), "seq").astype(jnp.float32),
        lax.psum(summed[2].astype(jnp.bfloat16), "seq").astype(jnp.float32),
        lax.psum(summed[3].astype(jnp.bfloat16), "seq").astype(jnp.float32),
        lax.psum(summed[4].astype(jnp.bfloat16), "seq").astype(jnp.float32),
        lax.psum(summed[5].astype(jnp.bfloat16), "seq").astype(jnp.float32),
        lax.psum(summed[6].astype(jnp.bfloat16), "seq").astype(jnp.float32),
        lax.psum(summed[7].astype(jnp.bfloat16), "seq").astype(jnp.float32),
        lax.psum(summed[8].astype(jnp.bfloat16), "seq").astype(jnp.float32),
        lax.psum(summed[9].astype(jnp.bfloat16), "seq").astype(jnp.float32),
        lax.psum(summed[10].astype(jnp.bfloat16), "seq").astype(jnp.float32),
        lax.psum(summed[11].astype(jnp.bfloat16), "seq").astype(jnp.float32),
        lax.psum(summed[12].astype(jnp.bfloat16), "seq").astype(jnp.float32),
        lax.psum(summed[13].astype(jnp.bfloat16), "seq").astype(jnp.float32),
        lax.psum(summed[14].astype(jnp.bfloat16), "seq").astype(jnp.float32),
        lax.psum(summed[15].astype(jnp.bfloat16), "seq").astype(jnp.float32),
        lax.psum(summed[16].astype(jnp.bfloat16), "seq").astype(jnp.float32),
        lax.psum(summed[17].astype(jnp.bfloat16), "seq").astype(jnp.float32),
        lax.psum(summed[18].astype(jnp.bfloat16), "seq").astype(jnp.float32),
        lax.psum(summed[19].astype(jnp.bfloat16), "seq").astype(jnp.float32),
        lax.psum(summed[20].astype(jnp.bfloat16), "seq").astype(jnp.float32),
        lax.psum(summed[21].astype(jnp.bfloat16), "seq").astype(jnp.float32),
        lax.psum(summed[22].astype(jnp.bfloat16), "seq").astype(jnp.float32),
        lax.psum(summed[23].astype(jnp.bfloat16), "seq").astype(jnp.float32),
    )
    finished = list(finished)
    return (hidden_out, hidden_grad, memory_grad) + tuple(finished)


def solution(mesh):
    in_specs = (
        P("dp", "seq", None),
        P("dp", "seq", None),
        P("dp", "seq"),
        P("dp", "seq"),
        P("dp", "seq", None),
        P(),
        P(),
        P(),
        P(),
        P(),
        P(),
        P(),
        P(),
        P(),
        P(),
        P(),
        P(),
        P(),
        P(),
        P(),
        P(),
        P(),
        P(),
        P(),
        P(),
        P(),
        P(),
        P(),
        P(),
    )
    out_specs = (
        P("dp", "seq", None),
        P("dp", "seq", None),
        P("dp", "seq", None),
        P("dp", None),
        P("dp"),
        P("dp", None),
        P("dp", None),
        P("dp"),
        P("dp", None),
        P("dp"),
        P("dp"),
        P("dp"),
        P("dp", None),
        P("dp"),
        P("dp", None),
        P("dp", None),
        P("dp"),
        P("dp", None),
        P("dp"),
        P("dp"),
        P("dp"),
        P("dp", None),
        P("dp"),
        P("dp", None),
        P("dp"),
        P("dp"),
        P("dp"),
    )
    return jax.shard_map(
        on_device, mesh=mesh, in_specs=in_specs, out_specs=out_specs, check_vma=False
    )
```

profile of v0, /device:TPU:0, one launch (start us, length us, event | category | flops | bytes accessed | tf_op | source)
XLA Modules:
  0.0 1531.7 jit_solution(308128519352585972)
XLA Ops:
  46.6 13.1 all-gather.7.cloned.1.call-done
  64.4 21.1 %fusion.6 = (f32[2,12,512]{2,1,0:T(8,128)S(1)}, f32[2,12,512,1024]{3,2,1,0:T(8,128)}) fusion(pred[2,512,1024]{2,1,0:T(8,128)(4,1)S(1)} %get-tuple-element.175, bf16[2,512,12,64]{1,3,2,0:T(8,128)(2,1)} %bitcast.210, bf16[2,1024,12,64]{1,3,2,0:T(8,128)(2,1)} %bitcast.202), kind=kOutput, calls=%fused_computation.18 | convolution fusion | flops 1648349184 | bytes 56147968 | tf_op jit(solution)/shard_map/rqhd,rkhd->rhqk/dot_general | solution.py:46
  85.5 22.3 %fusion.4 = f32[2,12,512]{2,1,0:T(8,128)S(1)} fusion(f32[2,12,512,1024]{3,2,1,0:T(8,128)} %get-tuple-element.177, f32[2,12,512]{2,1,0:T(8,128)S(1)} %get-tuple-element.176, pred[2,512,1024]{2,1,0:T(8,128)(4,1)S(1)} %get-tuple-element.175), kind=kLoop, calls=%fused_computation.16 | loop fusion | flops 50319360 | bytes 51478528 | tf_op jit(solution)/shard_map/reduce_sum | solution.py:60
  112.6 22.7 %fusion.110 = bf16[2,12,64,512]{3,2,1,0:T(8,128)(2,1)S(1)} fusion(bf16[2,1024,12,64]{1,3,2,0:T(8,128)(2,1)} %bitcast.198, f32[2,12,512,1024]{3,2,1,0:T(8,128)} %get-tuple-element.177, f32[2,12,512]{2,1,0:T(8,128)S(1)} %fusion.4, f32[2,12,512]{2,1,0:T(8,128)S(1)} %get-tuple-element.176, pred[2,512,1024]{2,1,0:T(8,128)(4,1)S(1)} %get-tuple-element.175), kind=kOutput, calls=%fused_computation.136 | convolution fusion | flops 1674313728 | bytes 56197120 | tf_op jit(solution)/shard_map/rhqk,rkhd->rqhd/dot_general | solution.py:62
  142.4 10.9 all-gather.11.cloned.1.call-done
  158.0 21.1 %fusion.7 = (f32[2,12,512]{2,1,0:T(8,128)S(1)}, f32[2,12,512,1024]{3,2,1,0:T(8,128)}) fusion(pred[2,512,1024]{2,1,0:T(8,128)(4,1)S(1)} %copy-done.5, bf16[2,512,12,64]{1,3,2,0:T(8,128)(2,1)} %bitcast.212, bf16[2,1024,12,64]{1,3,2,0:T(8,128)(2,1)} %bitcast.204), kind=kOutput, calls=%fused_computation.19 | convolution fusion | flops 1648349184 | bytes 56147968 | tf_op jit(solution)/shard_map/rqhd,rkhd->rhqk/dot_general | solution.py:46
  179.1 22.3 %fusion.5 = f32[2,12,512]{2,1,0:T(8,128)S(1)} fusion(f32[2,12,512,1024]{3,2,1,0:T(8,128)} %get-tuple-element.181, f32[2,12,512]{2,1,0:T(8,128)S(1)} %get-tuple-element.180, pred[2,512,1024]{2,1,0:T(8,128)(4,1)S(1)} %copy-done.5), kind=kLoop, calls=%fused_computation.17 | loop fusion | flops 50319360 | bytes 51478528 | tf_op jit(solution)/shard_map/reduce_sum | solution.py:60
  206.7 21.2 %fusion.109 = bf16[2,12,64,512]{3,2,1,0:T(8,128)(2,1)S(1)} fusion(bf16[2,1024,12,64]{1,3,2,0:T(8,128)(2,1)} %bitcast.200, f32[2,12,512,1024]{3,2,1,0:T(8,128)} %get-tuple-element.181, f32[2,12,512]{2,1,0:T(8,128)S(1)} %fusion.5, f32[2,12,512]{2,1,0:T(8,128)S(1)} %get-tuple-element.180, pred[2,512,1024]{2,1,0:T(8,128)(4,1)S(1)} %copy-done.5), kind=kOutput, calls=%fused_computation.135 | convolution fusion | flops 1674313728 | bytes 56197120 | tf_op jit(solution)/shard_map/rhqk,rkhd->rqhd/dot_general | solution.py:62
  230.8 15.2 fusion.84
  246.0 31.8 %multiply_convert_fusion.2 = (bf16[2,512,3072]{2,1,0:T(8,128)(2,1)S(1)}, f32[2,512,3072]{2,1,0:T(8,128)}) fusion(f32[2,512,3072]{2,1,0:T(8,128)} %get-tuple-element.184, f32[3072]{0:T(1024)S(1)} %copy-done.31, u8[512,3072]{1,0:T(8,128)(4,1)S(1)} %get-tuple-element.109, u8[512,3072]{1,0:T(8,128)(4,1)S(1)} %get-tuple-element.108), kind=kLoop, calls=%fused_computation.56 | loop fusion | flops 223346688 | bytes 34615296 | tf_op jit(solution)/shard_map/convert_element_type | solution.py:177
  277.9 10.0 fusion.179
  295.5 19.1 %fusion.186 = (bf16[3072]{0:T(1024)(128)(2,1)}, bf16[2,512,3072]{2,1,0:T(8,128)(2,1)}) fusion(f32[2,512,3072]{2,1,0:T(8,128)} %get-tuple-element.169, bf16[2,512,768]{2,1,0:T(8,128)(2,1)} %get-tuple-element.159, bf16[3072,768]{1,0:T(8,128)(2,1)} %param.54, f32[2,512,3072]{2,1,0:T(8,128)} %get-tuple-element.184, f32[3072]{0:T(1024)S(1)} %copy-done.31), kind=kOutput, calls=%fused_computation.211 | convolution fusion | flops 4882166784 | bytes 37767168 | tf_op jit(solution)/shard_map/rte,de->rtd/dot_general | solution.py:16
  314.6 11.4 multiply_reduce_fusion.2
  336.4 22.7 %fusion.87 = bf16[2,12,64,1024]{3,2,1,0:T(8,128)(2,1)} fusion(bf16[2,512,12,64]{1,3,2,0:T(8,128)(2,1)} %bitcast.208, f32[2,12,512,1024]{3,2,1,0:T(8,128)} %get-tuple-element.181, f32[2,12,512]{2,1,0:T(8,128)S(1)} %copy-done.29, pred[2,512,1024]{2,1,0:T(8,128)(4,1)S(1)} %copy-done.5), kind=kOutput, calls=%fused_computation.124 | convolution fusion | flops 1662517248 | bytes 56147968 | tf_op jit(solution)/shard_map/rhqk,rqhd->rkhd/dot_general | solution.py:72
  359.1 22.4 %fusion.187 = f32[2,12,512,1024]{3,2,1,0:T(8,128)} fusion(bf16[2,512,12,64]{1,3,2,0:T(8,128)(2,1)} %bitcast.209, bf16[2,1024,12,64]{1,3,2,0:T(8,128)(2,1)} %bitcast.201), kind=kOutput, calls=%fused_computation.212 | convolution fusion | flops 1610612736 | bytes 55050240 | tf_op jit(solution)/shard_map/rqhd,rkhd->rhqk/dot_general | solution.py:78
  381.5 83.7 %fusion.96 = bf16[2,12,64,1024]{3,2,1,0:T(8,128)(2,1)} fusion(bf16[2,512,12,64]{1,3,2,0:T(8,128)(2,1)} %bitcast.213, f32[2,12,512,1024]{3,2,1,0:T(8,128)} %fusion.187, f32[2,12,512,1024]{3,2,1,0:T(8,128)} %get-tuple-element.181, f32[2,12,512]{2,1,0:T(8,128)S(1)} %copy-done.29, pred[2,512,1024]{2,1,0:T(8,128)(4,1)S(1)} %copy-done.5), kind=kOutput, calls=%fused_computation.127 | convolution fusion | flops 1750610944 | bytes 106479616 | tf_op jit(solution)/shard_map/rhqk,rqhd->rkhd/dot_general | solution.py:87
  465.3 82.6 %fusion.183 = (bf16[12,64]{1,0:T(8,128)(2,1)}, bf16[2,12,64,512]{3,2,1,0:T(8,128)(2,1)}) fusion(bf16[2,1024,12,64]{1,3,2,0:T(8,128)(2,1)} %bitcast.205, f32[2,12,512,1024]{3,2,1,0:T(8,128)} %fusion.187, f32[2,12,512,1024]{3,2,1,0:T(8,128)} %get-tuple-element.181, f32[2,12,512]{2,1,0:T(8,128)S(1)} %copy-done.29, pred[2,512,1024]{2,1,0:T(8,128)(4,1)S(1)} %copy-done.5), kind=kOutput, calls=%fused_computation.210 | convolution fusion | flops 1750610176 | bytes 106481152 | tf_op jit(solution)/shard_map/rhqk,rkhd->rqhd/dot_general | solution.py:84
  565.2 22.9 %fusion.90 = bf16[2,12,64,1024]{3,2,1,0:T(8,128)(2,1)} fusion(bf16[2,512,12,64]{1,3,2,0:T(8,128)(2,1)} %bitcast.206, f32[2,12,512,1024]{3,2,1,0:T(8,128)} %get-tuple-element.177, f32[2,12,512]{2,1,0:T(8,128)S(1)} %log_add_fusion, pred[2,512,1024]{2,1,0:T(8,128)(4,1)S(1)} %copy-done.4), kind=kOutput, calls=%fused_computation.125 | convolution fusion | flops 1662517248 | bytes 56147968 | tf_op jit(solution)/shard_map/rhqk,rqhd->rkhd/dot_general | solution.py:72
  588.2 22.4 %fusion.188 = f32[2,12,512,1024]{3,2,1,0:T(8,128)} fusion(bf16[2,512,12,64]{1,3,2,0:T(8,128)(2,1)} %bitcast.207, bf16[2,1024,12,64]{1,3,2,0:T(8,128)(2,1)} %bitcast.199), kind=kOutput, calls=%fused_computation.213 | convolution fusion | flops 1610612736 | bytes 55050240 | tf_op jit(solution)/shard_map/rqhd,rkhd->rhqk/dot_general | solution.py:78
  610.6 83.7 %fusion.93 = bf16[2,12,64,1024]{3,2,1,0:T(8,128)(2,1)} fusion(bf16[2,512,12,64]{1,3,2,0:T(8,128)(2,1)} %bitcast.211, f32[2,12,512,1024]{3,2,1,0:T(8,128)} %fusion.188, f32[2,12,512,1024]{3,2,1,0:T(8,128)} %get-tuple-element.177, f32[2,12,512]{2,1,0:T(8,128)S(1)} %log_add_fusion, pred[2,512,1024]{2,1,0:T(8,128)(4,1)S(1)} %copy-done.4), kind=kOutput, calls=%fused_computation.126 | convolution fusion | flops 1750610944 | bytes 106479616 | tf_op jit(solution)/shard_map/rhqk,rqhd->rkhd/dot_general | solution.py:87
  694.4 82.0 %fusion.180 = (bf16[12,64]{1,0:T(8,128)(2,1)S(1)}, bf16[2,12,64,512]{3,2,1,0:T(8,128)(2,1)}) fusion(bf16[2,1024,12,64]{1,3,2,0:T(8,128)(2,1)} %bitcast.203, f32[2,12,512,1024]{3,2,1,0:T(8,128)} %fusion.188, f32[2,12,512,1024]{3,2,1,0:T(8,128)} %get-tuple-element.177, f32[2,12,512]{2,1,0:T(8,128)S(1)} %log_add_fusion, pred[2,512,1024]{2,1,0:T(8,128)(4,1)S(1)} %copy-done.4), kind=kOutput, calls=%fused_computation.209 | convolution fusion | flops 1750610176 | bytes 106481152 | tf_op jit(solution)/shard_map/rhqk,rkhd->rqhd/dot_general | solution.py:84
  815.4 10.5 bitcast_convert_fusion.1
  850.7 49.6 %reduce-scatter.51.cloned.1.call-done = bf16[48,768]{1,0:T(8,128)(2,1)} async-done(((bf16[768,768]{1,0:T(8,128)(2,1)}), bf16[48,768]{1,0:T(8,128)(2,1)}) %reduce-scatter.51.cloned.1.call-update) | async-done | bytes 73744
  902.0 59.1 %reduce-scatter.49.cloned.1.call-done = bf16[48,768]{1,0:T(8,128)(2,1)} async-done(((bf16[768,768]{1,0:T(8,128)(2,1)}), bf16[48,768]{1,0:T(8,128)(2,1)}) %reduce-scatter.49.cloned.1.call-update) | async-done | bytes 73744
  962.7 58.9 %reduce-scatter.47.cloned.1.call-done = bf16[48,768]{1,0:T(8,128)(2,1)} async-done(((bf16[768,768]{1,0:T(8,128)(2,1)}), bf16[48,768]{1,0:T(8,128)(2,1)}) %reduce-scatter.47.cloned.1.call-update) | async-done | bytes 73744
  1023.3 59.0 %reduce-scatter.45.cloned.1.call-done = bf16[48,768]{1,0:T(8,128)(2,1)} async-done(((bf16[768,768]{1,0:T(8,128)(2,1)}), bf16[48,768]{1,0:T(8,128)(2,1)}) %reduce-scatter.45.cloned.1.call-update) | async-done | bytes 73744
  1084.0 58.9 %reduce-scatter.37.cloned.1.call-done = bf16[48,768]{1,0:T(8,128)(2,1)} async-done(((bf16[768,768]{1,0:T(8,128)(2,1)}), bf16[48,768]{1,0:T(8,128)(2,1)}) %reduce-scatter.37.cloned.1.call-update) | async-done | bytes 73744 | tf_op jit(solution)/shard_map/reduce_scatter | solution.py:324
  1142.9 60.6 %reduce-scatter.35.cloned.1.call-done = bf16[48,768]{1,0:T(8,128)(2,1)} async-done(((bf16[768,768]{1,0:T(8,128)(2,1)}), bf16[48,768]{1,0:T(8,128)(2,1)}) %reduce-scatter.35.cloned.1.call-update) | async-done | bytes 73744 | tf_op jit(solution)/shard_map/reduce_scatter | solution.py:309
  1203.5 61.1 %reduce-scatter.33.cloned.1.call-done = bf16[48,768]{1,0:T(8,128)(2,1)} async-done(((bf16[768,768]{1,0:T(8,128)(2,1)}), bf16[48,768]{1,0:T(8,128)(2,1)}) %reduce-scatter.33.cloned.1.call-update) | async-done | bytes 73744 | tf_op jit(solution)/shard_map/reduce_scatter | solution.py:297
  1264.6 78.3 %reduce-scatter.39.cloned.1.call-done = bf16[48,3072]{1,0:T(8,128)(2,1)} async-done(((bf16[768,3072]{1,0:T(8,128)(2,1)}), bf16[48,3072]{1,0:T(8,128)(2,1)}) %reduce-scatter.39.cloned.1.call-update) | async-done | bytes 294928 | tf_op jit(solution)/shard_map/reduce_scatter | solution.py:336
  1342.9 78.8 %reduce-scatter.41.cloned.1.call-done = bf16[192,768]{1,0:T(8,128)(2,1)} async-done(((bf16[3072,768]{1,0:T(8,128)(2,1)}), bf16[192,768]{1,0:T(8,128)(2,1)}) %reduce-scatter.41.cloned.1.call-update) | async-done | bytes 294928 | tf_op jit(solution)/shard_map/reduce_scatter | solution.py:342
  1429.3 58.1 %all-reduce.14 = (bf16[768]{0:T(1024)(128)(2,1)S(1)}, bf16[768]{0:T(1024)(128)(2,1)S(1)}, bf16[768]{0:T(1024)(128)(2,1)S(1)}, bf16[768]{0:T(1024)(128)(2,1)S(1)}...) all-reduce(bf16[768]{0:T(1024)(128)(2,1)S(1)} %reduce_sum.366, ...), channel_id=7, replica_groups=mesh['dp'=16,'seq'=2] {'dp'}, use_global_device_ids=true, to_apply=%region_25.26.clone | all-reduce | flops 13056 | bytes 52224
  (364 shorter events, 217.3 us)
Async XLA Ops:
  7.2 52.5 %all-gather.7.cloned.1.call-start = ((), (), s32[]{:S(2)}) async-start(), calls=%async_computation.15 | async-start | bytes 4718592 | tf_op jit(solution)/shard_map/all_gather | solution.py:132
  11.8 96.0 %all-gather.5.cloned.1.call-start = ((), (), s32[]{:S(2)}) async-start(), calls=%async_computation.14 | async-start | bytes 4718592 | tf_op jit(solution)/shard_map/all_gather | solution.py:133
  15.9 137.4 %all-gather.11.cloned.1.call-start = ((), (), s32[]{:S(2)}) async-start(), calls=%async_computation.17 | async-start | bytes 4718592 | tf_op jit(solution)/shard_map/all_gather | solution.py:141
  19.9 182.1 %all-gather.9.cloned.1.call-start = ((), (), s32[]{:S(2)}) async-start(), calls=%async_computation.16 | async-start | bytes 4718592 | tf_op jit(solution)/shard_map/all_gather | solution.py:142
  22.8 758.4 %reduce-scatter.31.cloned.1.call-start = ((), (), s32[]{:S(2)}) async-start(), calls=%async_computation.21 | async-start | bytes 4718592 | tf_op jit(solution)/shard_map/reduce_scatter | solution.py:208
  28.2 199.8 %copy-start.41 = (f32[768]{0:T(1024)}, f32[768]{0:T(1024)S(1)}, u32[]{:S(2)}) copy-start(f32[768]{0:T(1024)S(1)} %convert_element_type.419) | copy-start | bytes 9220
  29.4 198.6 %copy-start.61 = (f32[768]{0:T(1024)}, f32[768]{0:T(1024)S(1)}, u32[]{:S(2)}) copy-start(f32[768]{0:T(1024)S(1)} %convert_element_type.420) | copy-start | bytes 9220
  46.6 66.0 %copy-start.3 = (pred[2,512,1024]{2,1,0:T(8,128)(4,1)}, pred[2,512,1024]{2,1,0:T(8,128)(4,1)S(1)}, u32[]{:S(2)}) copy-start(pred[2,512,1024]{2,1,0:T(8,128)(4,1)S(1)} %get-tuple-element.175) | copy-start | bytes 3145732
  85.5 27.0 %copy-start.22 = (f32[2,12,512]{2,1,0:T(8,128)}, f32[2,12,512]{2,1,0:T(8,128)S(1)}, u32[]{:S(2)}) copy-start(f32[2,12,512]{2,1,0:T(8,128)S(1)} %get-tuple-element.176) | copy-start | bytes 147460
  137.0 90.9 %copy-start.32 = (f32[2,512]{1,0:T(2,128)}, f32[2,512]{1,0:T(2,128)S(1)}, u32[]{:S(2)}) copy-start(f32[2,512]{1,0:T(2,128)S(1)} %broadcast_multiply_fusion.2) | copy-start | bytes 12292
  139.1 88.8 %copy-start.44 = (f32[2,512]{1,0:T(2,128)}, f32[2,512]{1,0:T(2,128)S(1)}, u32[]{:S(2)}) copy-start(f32[2,512]{1,0:T(2,128)S(1)} %fusion.139) | copy-start | bytes 12292
  230.0 47.8 %copy-start.10 = (f32[2,512,768]{2,1,0:T(8,128)}, f32[2,512,768]{2,1,0:T(8,128)S(1)}, u32[]{:S(2)}) copy-start(f32[2,512,768]{2,1,0:T(8,128)S(1)} %get-tuple-element.183) | copy-start | bytes 9437188
  230.0 96.0 %copy-start.35 = (f32[2,512]{1,0:T(2,128)}, f32[2,512]{1,0:T(2,128)S(1)}, u32[]{:S(2)}) copy-start(f32[2,512]{1,0:T(2,128)S(1)} %broadcast_multiply_fusion.1) | copy-start | bytes 12292
  230.8 95.2 %copy-start.47 = (f32[2,512]{1,0:T(2,128)}, f32[2,512]{1,0:T(2,128)S(1)}, u32[]{:S(2)}) copy-start(f32[2,512]{1,0:T(2,128)S(1)} %fusion.140) | copy-start | bytes 12292
  246.0 31.9 %copy-start.64 = (f32[768]{0:T(1024)S(1)}, f32[768]{0:T(1024)}, u32[]{:S(2)}) copy-start(f32[768]{0:T(1024)} %convert_element_type.438) | copy-start | bytes 9220
  359.1 426.4 %reduce-scatter.29.cloned.1.call-start = ((), (), s32[]{:S(2)}) async-start(), calls=%async_computation.20 | async-start | bytes 4718592 | tf_op jit(solution)/shard_map/reduce_scatter | solution.py:205
  465.2 82.7 %copy-start.33 = (f32[2,512]{1,0:T(2,128)S(1)}, f32[2,512]{1,0:T(2,128)}, u32[]{:S(2)}) copy-start(f32[2,512]{1,0:T(2,128)} %copy-done.32) | copy-start | bytes 12292
  465.2 82.7 %copy-start.42 = (f32[768]{0:T(1024)S(1)}, f32[768]{0:T(1024)}, u32[]{:S(2)}) copy-start(f32[768]{0:T(1024)} %copy-done.41) | copy-start | bytes 9220
  465.3 82.6 %copy-start.45 = (f32[2,512]{1,0:T(2,128)S(1)}, f32[2,512]{1,0:T(2,128)}, u32[]{:S(2)}) copy-start(f32[2,512]{1,0:T(2,128)} %copy-done.44) | copy-start | bytes 12292
  465.3 324.6 %reduce-scatter.27.cloned.1.call-start = ((), (), s32[]{:S(2)}) async-start(), calls=%async_computation.19 | async-start | bytes 4718592 | tf_op jit(solution)/shard_map/reduce_scatter | solution.py:237
  588.1 206.8 %reduce-scatter.25.cloned.1.call-start = ((), (), s32[]{:S(2)}) async-start(), calls=%async_computation.18 | async-start | bytes 4718592 | tf_op jit(solution)/shard_map/reduce_scatter | solution.py:234
  694.3 150.4 %reduce-scatter.43.cloned.1.call-start = ((), (), s32[]{:S(2)}) async-start(), calls=%async_computation.27 | async-start | bytes 1253376
  781.1 119.2 %reduce-scatter.51.cloned.1.call-start = ((), (), s32[]{:S(2)}) async-start(), calls=%async_computation.31 | async-start | bytes 1253376
  785.5 175.6 %reduce-scatter.49.cloned.1.call-start = ((), (), s32[]{:S(2)}) async-start(), calls=%async_computation.30 | async-start | bytes 1253376
  789.8 231.8 %reduce-scatter.47.cloned.1.call-start = ((), (), s32[]{:S(2)}) async-start(), calls=%async_computation.29 | async-start | bytes 1253376
  794.7 287.6 %reduce-scatter.45.cloned.1.call-start = ((), (), s32[]{:S(2)}) async-start(), calls=%async_computation.28 | async-start | bytes 1253376
  801.9 341.0 %reduce-scatter.37.cloned.1.call-start = ((), (), s32[]{:S(2)}) async-start(), calls=%async_computation.24 | async-start | bytes 1253376 | tf_op jit(solution)/shard_map/reduce_scatter | solution.py:324
  805.8 397.6 %reduce-scatter.35.cloned.1.call-start = ((), (), s32[]{:S(2)}) async-start(), calls=%async_computation.23 | async-start | bytes 1253376 | tf_op jit(solution)/shard_map/reduce_scatter | solution.py:309
  811.4 453.2 %reduce-scatter.33.cloned.1.call-start = ((), (), s32[]{:S(2)}) async-start(), calls=%async_computation.22 | async-start | bytes 1253376 | tf_op jit(solution)/shard_map/reduce_scatter | solution.py:297
  815.3 527.7 %reduce-scatter.39.cloned.1.call-start = ((), (), s32[]{:S(2)}) async-start(), calls=%async_computation.25 | async-start | bytes 5013504 | tf_op jit(solution)/shard_map/reduce_scatter | solution.py:336
  825.9 595.8 %reduce-scatter.41.cloned.1.call-start = ((), (), s32[]{:S(2)}) async-start(), calls=%async_computation.26 | async-start | bytes 5013504 | tf_op jit(solution)/shard_map/reduce_scatter | solution.py:342
  837.0 671.8 %all-reduce.19.cloned.1.call-start = ((), (), s32[]{:S(2)}) async-start(), calls=%async_computation.32 | async-start | bytes 3588096 | tf_op jit(solution)/shard_map/psum | solution.py:356
  (81 other events, 508.6 us)
Sparse Core Ops, SparseCore 0:
  12.0 47.7 all-gather.6
  61.8 44.9 all-gather.4
  108.3 44.9 all-gather.10
  155.3 44.9 all-gather.8
  359.2 43.6 reduce-scatter.30
  465.4 43.6 reduce-scatter.28
  588.3 43.6 reduce-scatter.26
  694.4 43.7 reduce-scatter.24
  781.2 58.4 reduce-scatter.42
  843.2 57.0 reduce-scatter.50
  903.9 57.0 reduce-scatter.48
  964.5 57.0 reduce-scatter.46
  1025.2 57.0 reduce-scatter.44
  1085.8 57.0 reduce-scatter.36
  1146.4 57.0 reduce-scatter.34
  1207.5 57.0 reduce-scatter.32
  1268.3 74.5 reduce-scatter.38
  1347.1 74.5 reduce-scatter.40
  1425.2 56.9 all-reduce.18
where the time goes:
time: 1540 us; the launch traced here: 1530 us
  matrix products  673 us (44%)
  waiting for transfers between devices  589 us (38%)
  other arithmetic  113 us (7%)
  blocking collectives  72.9 us (5%)
  local copies, waits for them, and re-layouts  65.4 us (4%)
  between operations  17 us (1%)
    unnamed x24, waiting for transfers between devices  227 us
    dot_general x2, matrix products, attend_backward(): jnp.einsum('rhqk,rqhd->rkhd', score_grads, split_heads(queries), preferre...  167 us
    dot_general x2, matrix products, attend_backward(): jnp.einsum('rhqk,rkhd->rqhd', score_grads, split_heads(key_rows), preferr...  165 us
    reduce_scatter x1, waiting for transfers between devices, on_device(): lax.psum_scatter(partial_grads[20].astype(jnp.bfloat16), 'dp', scatter_di...  78.8 us
    reduce_scatter x1, waiting for transfers between devices, on_device(): lax.psum_scatter(partial_grads[18].astype(jnp.bfloat16), 'dp', scatter_di...  78.3 us
    dot_general x10, matrix products, project_back(): jnp.einsum('rte,de->rtd', gradient, weight, preferred_element_type=jnp.fl...  65.1 us
    reduce_scatter x1, waiting for transfers between devices, on_device(): lax.psum_scatter(partial_grads[5].astype(jnp.bfloat16), 'dp', scatter_dim...  61.1 us
    reduce_scatter x1, waiting for transfers between devices, on_device(): lax.psum_scatter(partial_grads[9].astype(jnp.bfloat16), 'dp', scatter_dim...  60.6 us
  transfers between devices with their start and end apart: 19, of which 11 were waited for; matrix products, arithmetic and copies ran while one was open for 44% of the time, Pallas kernels for 0%

commit v1 on v0

--- a/solution.py
+++ b/solution.py
@@ -1,11 +1,138 @@
+import functools
 import math
 
 import jax
 import jax.numpy as jnp
 from jax import lax
+from jax.experimental import pallas as pl
+from jax.experimental.pallas import tpu as pltpu
 from jax.sharding import PartitionSpec as P
 
 HEADS = 12
+BF=jnp.bfloat16; F32=jnp.float32
+BIG=-1e30
+def dot(a,b): return jnp.dot(a,b,preferred_element_type=F32)
+
+def lane_low(shape): return lax.broadcasted_iota(jnp.int32, shape, 1) < 64
+
+def masks(seg_q, seg_k):
+    T=seg_q.shape[0]; K=seg_k.shape[0]
+    r=jnp.arange(64)[:,None]
+    oh=((r==seg_q[None,:])).astype(BF)
+    c=jnp.arange(128)[None,:]%64
+    mk=jnp.where(c<4, jnp.where(c==seg_k[:,None],0.0,BIG), jnp.where(c<7,-1.0,0.0)).astype(BF)
+    return oh,mk
+
+def fwd_kernel(q_ref,k_ref,v_ref,oh_ref,mk_ref,o_ref,l_ref,*,bq,causal):
+    T=q_ref.shape[0]; K=k_ref.shape[0]
+    low=lane_low((K,128))
+    qT=(q_ref[...]*BF(0.125)).T
+    vT=v_ref[...].T
+    k=k_ref[...]; mk=mk_ref[...]; oh=oh_ref[...]
+    ones=jnp.ones((16,K),BF)
+    if causal:
+        dm=lax.broadcasted_iota(jnp.int32,(bq,bq),0)<=lax.broadcasted_iota(jnp.int32,(bq,bq),1)
+    kas=[jnp.where(low,k,mk),jnp.where(low,mk,k)]
+    vas=[jnp.concatenate([vT[64*h:64*h+64],ones],0) for h in (0,1)]
+    qas=[jnp.concatenate([qT[:64],oh],0),jnp.concatenate([oh,qT[64:]],0)]
+    for i in range(T//bq):
+        os=[]
+        for h in (0,1):
+            qa=qas[h][:,i*bq:(i+1)*bq]
+            if causal:
+                s1=jnp.where(dm,dot(kas[h][i*bq:(i+1)*bq],qa),BIG)
+                m=jnp.max(s1,axis=0,keepdims=True)
+                if i:
+                    s0=dot(kas[h][:i*bq],qa)
+                    m=jnp.maximum(m,jnp.max(s0,axis=0,keepdims=True))
+                    o=dot(vas[h][:,:i*bq],jnp.exp(s0-m).astype(BF))
+                    o=o+dot(vas[h][:,i*bq:(i+1)*bq],jnp.exp(s1-m).astype(BF))
+                else:
+                    o=dot(vas[h][:,i*bq:(i+1)*bq],jnp.exp(s1-m).astype(BF))
+            else:
+                s=dot(kas[h],qa)
+                m=jnp.max(s,axis=0,keepdims=True)
+                o=dot(vas[h],jnp.exp(s-m).astype(BF))
+            l=o[64:65]
+            os.append(o[:64]/l)
+            l_ref[0,h:h+1,i*bq:(i+1)*bq]=m+jnp.log(l)
+        o_ref[i*bq:(i+1)*bq,:]=jnp.concatenate(os,0).T.astype(BF)
+
+def attend_fwd(q,k,v,oh,mk,causal,bq=256):
+    T,D=q.shape; K=k.shape[0]; n=D//128
+    pair=lambda r:pl.BlockSpec((r,128),lambda p:(0,p))
+    return pl.pallas_call(functools.partial(fwd_kernel,bq=bq,causal=causal),grid=(n,),
+        in_specs=[pair(T),pair(K),pair(K),pl.BlockSpec((64,T),lambda p:(0,0)),pl.BlockSpec((K,128),lambda p:(0,0))],
+        out_specs=[pair(T),pl.BlockSpec((1,8,T),lambda p:(p,0,0))],
+        out_shape=[jax.ShapeDtypeStruct((T,D),BF),jax.ShapeDtypeStruct((n,8,T),F32)],
+        name="attend_fwd",
+        compiler_params=pltpu.CompilerParams(vmem_limit_bytes=56*2**20))(q,k,v,oh,mk)
+
+def split3(x):
+    a=x.astype(BF); r=x-a.astype(F32); b=r.astype(BF); c=(r-b.astype(F32)).astype(BF)
+    return a,b,c
+
+def bwd_kernel(q_ref,k_ref,v_ref,do_ref,o_ref,l_ref,oh_ref,mk_ref,dq_ref,dk_ref,dv_ref,acc_ref,*,bk,causal):
+    T=q_ref.shape[0]; K=k_ref.shape[0]
+    low=lane_low((K,128))
+    lowt=lane_low((T,128))
+    q=q_ref[...]*BF(0.125); do=do_ref[...]
+    qT=q.T; doT=do.T
+    k=k_ref[...]; mk=mk_ref[...]; oh=oh_ref[...]; v=v_ref[...]
+    kT=k.T
+    prodT=(do.astype(F32)*o_ref[...].astype(F32)).T
+    rowi=lax.broadcasted_iota(jnp.int32,(64,T),0)
+    one=jnp.full((K,128),-1.0,BF)
+    if causal:
+        dm=lax.broadcasted_iota(jnp.int32,(bk,bk),0)<=lax.broadcasted_iota(jnp.int32,(bk,bk),1)
+    qas=[];das=[]
+    for h in (0,1):
+        L=l_ref[0,h:h+1,:]
+        a,b,c=split3(L)
+        ohl=jnp.where(rowi==4,a,jnp.where(rowi==5,b,jnp.where(rowi==6,c,oh)))
+        D=jnp.sum(prodT[64*h:64*h+64],axis=0,keepdims=True)
+        a,b,c=split3(D)
+        z=jnp.zeros((64,T),BF)
+        dd=jnp.where(rowi==0,a,jnp.where(rowi==1,b,jnp.where(rowi==2,c,z)))
+        if h==0:
+            qas.append(jnp.concatenate([qT[:64],ohl],0)); das.append(jnp.concatenate([doT[:64],dd],0))
+        else:
+            qas.append(jnp.concatenate([ohl,qT[64:]],0)); das.append(jnp.concatenate([dd,doT[64:]],0))
+    kas=[jnp.where(low,k,mk),jnp.where(low,mk,k)]
+    vas=[jnp.where(low,v,one),jnp.where(low,one,v)]
+    for j in range(K//bk):
+        dks=[];dvs=[]
+        q0=j*bk if causal else 0
+        ks=slice(j*bk,(j+1)*bk)
+        for h in (0,1):
+            s=dot(kas[h][ks],qas[h][:,q0:])
+            if causal:
+                sd=jnp.where(dm,s[:,:bk],BIG)
+                s=jnp.concatenate([sd,s[:,bk:]],1) if q0+bk<T else sd
+            p=jnp.exp(s)
+            dp=dot(vas[h][ks],das[h][:,q0:])
+            ds=(p*dp).astype(BF)
+            dvs.append(dot(p.astype(BF),do[q0:]))
+            dks.append(dot(ds,q[q0:]))
+            dqt=dot(kT[64*h:64*h+64,ks],ds)
+            if j==0: acc_ref[64*h:64*h+64,:]=dqt
+            else: acc_ref[64*h:64*h+64,q0:]+=dqt
+        lw=low[:bk]
+        dk_ref[ks,:]=jnp.where(lw,dks[0],dks[1]).astype(BF)
+        dv_ref[ks,:]=jnp.where(lw,dvs[0],dvs[1]).astype(BF)
+    dq_ref[...]=(acc_ref[...]*0.125).T.astype(BF)
+
+def attend_bwd(q,k,v,do,o,l,oh,mk,causal,bk=256,p0=0,np_=None):
+    T,D=q.shape; K=k.shape[0]; n=np_ or D//128
+    pin=lambda r:pl.BlockSpec((r,128),lambda p:(0,p+p0))
+    po=lambda r:pl.BlockSpec((r,128),lambda p:(0,p))
+    return pl.pallas_call(functools.partial(bwd_kernel,bk=bk,causal=causal),grid=(n,),
+        in_specs=[pin(T),pin(K),pin(K),pin(T),pin(T),pl.BlockSpec((1,8,T),lambda p:(p+p0,0,0)),pl.BlockSpec((64,T),lambda p:(0,0)),pl.BlockSpec((K,128),lambda p:(0,0))],
+        out_specs=[po(T),po(K),po(K)],
+        out_shape=[jax.ShapeDtypeStruct((T,128*n),BF),jax.ShapeDtypeStruct((K,128*n),BF),jax.ShapeDtypeStruct((K,128*n),BF)],
+        scratch_shapes=[pltpu.VMEM((128,T),F32)],
+        name="attend_bwd",
+        compiler_params=pltpu.CompilerParams(vmem_limit_bytes=56*2**20))(q,k,v,do,o,l,oh,mk)
 
 
 def project(values, weight):
@@ -90,7 +217,7 @@
     return (merge_heads(query_grads), merge_heads(key_terms), merge_heads(value_terms))
 
 
-def on_device(
+def split_rows(
     hidden_in,
     memory,
     tgt_segment,
@@ -382,6 +509,166 @@
     return (hidden_out, hidden_grad, memory_grad) + tuple(finished)
 
 
+def swap(block, ax, bit, size):
+    return lax.ppermute(block, ax, [(i, i ^ bit) for i in range(size)])
+
+
+def two(s, first, second):
+    return jnp.where(s == 0, jnp.concatenate([first, second], 0), jnp.concatenate([second, first], 0))
+
+
+def pick(array, index, axis):
+    return lax.dynamic_index_in_dim(array, index, axis, keepdims=False)
+
+
+def row_in(array, s):
+    own = pick(array, s, 0)
+    other = swap(pick(array, 1 - s, 0), "seq", 1, 2)
+    return two(s, own, other)
+
+
+def row_out(array, s):
+    half = array.shape[0] // 2
+    parts = array.reshape(2, half, array.shape[1])
+    own = pick(parts, s, 0)
+    other = swap(pick(parts, 1 - s, 0), "seq", 1, 2)
+    return two(s, own[None], other[None])
+
+
+def reduce_group(group):
+    dp = lax.axis_index("dp")
+    c, x, zl, zh = dp % 2, (dp // 2) % 2, (dp // 4) % 2, dp // 8
+    rest = group.shape[1:]
+    g = group.reshape((2, 2, 2, 2) + rest)
+    mine, got = pick(g, c, 3), swap(pick(g, 1 - c, 3), "dp", 1, 16)
+
+    def halves(mine, got, at, axis):
+        send = pick(mine, 1 - at, axis) + pick(got, 1 - at, axis)
+        keep = pick(mine, at, axis) + pick(got, at, axis)
+        return keep, send
+
+    keep, send = halves(mine, got, x, 2)
+    got = swap(send, "dp", 2, 16)
+    keep, send = halves(keep, got, zl, 1)
+    got = swap(send, "dp", 4, 16)
+    keep, send = halves(keep, got, zh, 0)
+    total = keep + swap(send, "dp", 8, 16)
+    return total + swap(total, "seq", 1, 2)
+
+
+def wgrad(values, gradient):
+    return lax.dot_general(values, gradient, (((0,), (0,)), ((), ())), preferred_element_type=jnp.float32)
+
+
+def back(gradient, weight):
+    return lax.dot_general(gradient, weight, (((1,), (1,)), ((), ())), preferred_element_type=jnp.float32)
+
+
+def col_sum(values):
+    return jnp.sum(values.astype(jnp.float32), axis=0)
+
+
+def whole_rows(
+    hidden_in, memory, tgt_segment, src_segment, out_grad,
+    self_query, query_bias, self_key, self_value, value_bias, self_output, output_bias,
+    first_gain, first_shift,
+    cross_query, cross_query_bias, cross_key, cross_value, cross_value_bias, cross_output,
+    cross_output_bias, second_gain, second_shift,
+    ffn_in, ffn_in_bias, ffn_out, ffn_out_bias, third_gain, third_shift,
+):
+    f32 = lambda v: v.astype(jnp.float32)
+    s = lax.axis_index("seq")
+    hidden = row_in(hidden_in, s)
+    segs = jnp.stack([tgt_segment, src_segment], -1)
+    segs = row_in(segs, s)
+    source = row_in(memory, s)
+    cotangent = row_in(out_grad, s)
+    tgt, src = segs[:, 0], segs[:, 1]
+    self_oh, self_mk = masks(tgt, tgt)
+    _, cross_mk = masks(tgt, src)
+    queries = (project(hidden, self_query) + f32(query_bias)).astype(BF)
+    key_rows = project(hidden, self_key).astype(BF)
+    value_rows = (project(hidden, self_value) + f32(value_bias)).astype(BF)
+    memory_keys = project(source, cross_key).astype(BF)
+    memory_values = (project(source, cross_value) + f32(cross_value_bias)).astype(BF)
+    self_mixed, self_totals = attend_fwd(queries, key_rows, value_rows, self_oh, self_mk, True, 512)
+    self_branch = project(self_mixed, self_output) + f32(output_bias)
+    first_norm, first_pull = jax.vjp(layer_norm, f32(hidden) + self_branch, f32(first_gain), f32(first_shift))
+    first_low = first_norm.astype(BF)
+    cross_queries = (project(first_low, cross_query) + f32(cross_query_bias)).astype(BF)
+    cross_mixed, cross_totals = attend_fwd(cross_queries, memory_keys, memory_values, self_oh, cross_mk, False, 512)
+    cross_branch = project(cross_mixed, cross_output) + f32(cross_output_bias)
+    second_norm, second_pull = jax.vjp(layer_norm, first_norm + cross_branch, f32(second_gain), f32(second_shift))
+    second_low = second_norm.astype(BF)
+    inner_rows = project(second_low, ffn_in) + f32(ffn_in_bias)
+    activation_full, gelu_pull = jax.vjp(exact_gelu, inner_rows)
+    activation = activation_full.astype(BF)
+    ffn_branch = project(activation, ffn_out) + f32(ffn_out_bias)
+    final_norm, third_pull = jax.vjp(layer_norm, second_norm + ffn_branch, f32(third_gain), f32(third_shift))
+    hidden_out = row_out(final_norm.astype(BF), s)
+    third_back, grad_third_gain, grad_third_shift = third_pull(f32(cotangent))
+    ffn_back = third_back.astype(BF)
+    pieces = lambda v: v.astype(BF).reshape((16, v.shape[0] // 16) + v.shape[1:])
+    total_ffn_out = reduce_group(pieces(wgrad(activation, ffn_back)))
+    activation_back = back(ffn_back, ffn_out)
+    inner_back = gelu_pull(activation_back)[0].astype(BF)
+    total_ffn_in = reduce_group(pieces(wgrad(second_low, inner_back)))
+    second_back, grad_second_gain, grad_second_shift = second_pull(third_back + back(inner_back, ffn_in))
+    cross_back = second_back.astype(BF)
+    cross_mixed_back = back(cross_back, cross_output).astype(BF)
+    cross_query_back, memory_key_back, memory_value_back = attend_bwd(
+        cross_queries, memory_keys, memory_values, cross_mixed_back, cross_mixed, cross_totals, self_oh, cross_mk, False, 512
+    )
+    cross_group = jnp.concatenate(
+        [
+            pieces(wgrad(cross_mixed, cross_back)),
+            pieces(wgrad(first_low, cross_query_back)),
+            pieces(wgrad(source, memory_key_back)),
+            pieces(wgrad(source, memory_value_back)),
+        ],
+        1,
+    )
+    total_cross = reduce_group(cross_group)
+    memory_grad = row_out((back(memory_key_back, cross_key) + back(memory_value_back, cross_value)).astype(BF), s)
+    first_back, grad_first_gain, grad_first_shift = first_pull(second_back + back(cross_query_back, cross_query))
+    self_back = first_back.astype(BF)
+    self_mixed_back = back(self_back, self_output).astype(BF)
+    query_back, key_back, value_back = attend_bwd(
+        queries, key_rows, value_rows, self_mixed_back, self_mixed, self_totals, self_oh, self_mk, True, 256
+    )
+    hidden_grad = row_out(
+        (first_back + back(query_back, self_query) + back(key_back, self_key) + back(value_back, self_value)).astype(BF), s
+    )
+    vectors = [
+        col_sum(query_back), col_sum(value_back), col_sum(self_back), grad_first_gain, grad_first_shift,
+        col_sum(cross_query_back), col_sum(memory_value_back), col_sum(cross_back),
+        grad_second_gain, grad_second_shift, col_sum(ffn_back), grad_third_gain, grad_third_shift,
+        col_sum(inner_back),
+    ]
+    flat = jnp.concatenate([v.astype(BF).reshape(16, -1) for v in vectors], 1)
+    flat = jnp.pad(flat, ((0, 0), (0, 16 * 768 - flat.shape[1]))).reshape(16, 16, 768)
+    self_group = jnp.concatenate(
+        [
+            pieces(wgrad(hidden, query_back)),
+            pieces(wgrad(hidden, key_back)),
+            pieces(wgrad(hidden, value_back)),
+            pieces(wgrad(self_mixed, self_back)),
+            flat,
+        ],
+        1,
+    )
+    total_self = reduce_group(self_group)
+    g = lambda total, i: f32(total[48 * i : 48 * i + 48])
+    tail = f32(total_self[192:]).reshape(-1)
+    v = [tail[48 * i : 48 * i + 48] for i in range(13)] + [tail[48 * 13 : 48 * 13 + 192]]
+    return (
+        hidden_out, hidden_grad, memory_grad,
+        g(total_self, 0), v[0], g(total_self, 1), g(total_self, 2), v[1], g(total_self, 3), v[2], v[3], v[4],
+        g(total_cross, 1), v[5], g(total_cross, 2), g(total_cross, 3), v[6], g(total_cross, 0), v[7], v[8], v[9],
+        f32(total_ffn_in), v[13], f32(total_ffn_out), v[10], v[11], v[12],
+    )
+
+
 def solution(mesh):
     in_specs = (
         P("dp", "seq", None),
@@ -443,6 +730,13 @@
         P("dp"),
         P("dp"),
     )
+    rows_form = mesh.shape["seq"] == 2 and mesh.shape["dp"] == 16
+
+    def on_device(*arrays):
+        if rows_form and arrays[0].shape[0] == 2:
+            return whole_rows(*arrays)
+        return split_rows(*arrays)
+
     return jax.shard_map(
         on_device, mesh=mesh, in_specs=in_specs, out_specs=out_specs, check_vma=False
     )

time: 1540 us -> 523 us (0.34)
  matrix products: 673 us -> 155 us
  waiting for transfers between devices: 589 us -> 124 us
  Pallas kernels: 0 us -> 103 us
  blocking collectives: 72.9 us -> 0 us
  other arithmetic: 113 us -> 68.3 us
  local copies, waits for them, and re-layouts: 65.4 us -> 34 us
  starting transfers between devices: 1.25 us -> 32.5 us
    dot_general x32 -> x20, matrix products: 623 us -> 84.1 us  [the longest x10 43.1 us: back(): lax.dot_general(gradient, weight, (((1,), (1,)), ((), ())), preferred_ele...]
    reduce_scatter x9 -> x0, waiting for transfers between devices: 338 us -> none  [the longest x1 78.8 us: on_device(): lax.psum_scatter(partial_grads[20].astype(jnp.bfloat16), 'dp', scatter_di...]
    unnamed x24 -> x0, waiting for transfers between devices: 227 us -> none
    ppermute x0 -> x27, waiting for transfers between devices: none -> 124 us  [swap(): return lax.ppermute(block, ax, [(i, i ^ bit) for i in range(size)])]
    pallas_call x0 -> x4, Pallas kernels: none -> 103 us  [the longest x2 59.3 us: attend_bwd(): pl.pallas_call(functools.partial(bwd_kernel, bk=bk, causal=causal), grid=...]
    unnamed x1 -> x0, blocking collectives: 58.1 us -> none
    reduce_sum x7, other arithmetic: 51.4 us -> 6.45 us  [col_sum(): return jnp.sum(values.astype(jnp.float32), axis=0)]
    ppermute x0 -> x27, starting transfers between devices: none -> 32.5 us  [swap(): return lax.ppermute(block, ax, [(i, i ^ bit) for i in range(size)])]
  transfers between devices with their start and end apart: 19 -> 27, of which waited for: 11 -> 11; matrix products, arithmetic and copies ran while one was open for 44% -> 32% of each run, Pallas kernels for 0% -> 13%
where the time goes in v1:
time: 523 us; the launch traced here: 518 us
  matrix products  155 us (30%)
  waiting for transfers between devices  124 us (24%)
  Pallas kernels  103 us (20%)
  other arithmetic  68.3 us (13%)
  local copies, waits for them, and re-layouts  34 us (7%)
  starting transfers between devices  32.5 us (6%)
    ppermute x27, waiting for transfers between devices, swap(): return lax.ppermute(block, ax, [(i, i ^ bit) for i in range(size)])  124 us
    dot_general x10, matrix products, project(): return jnp.dot(values, weight, preferred_element_type=jnp.float32)  70.9 us
    pallas_call x2, Pallas kernels, attend_bwd(): pl.pallas_call(functools.partial(bwd_kernel, bk=bk, causal=causal), grid=...  59.3 us
    pallas_call x2, Pallas kernels, attend_fwd(): pl.pallas_call(functools.partial(fwd_kernel, bq=bq, causal=causal), grid=...  43.7 us
    dot_general x10, matrix products, back(): lax.dot_general(gradient, weight, (((1,), (1,)), ((), ())), preferred_ele...  43.1 us
    dot_general x10, matrix products, wgrad(): lax.dot_general(values, gradient, (((0,), (0,)), ((), ())), preferred_ele...  41 us
    ppermute x27, starting transfers between devices, swap(): return lax.ppermute(block, ax, [(i, i ^ bit) for i in range(size)])  32.5 us
    add x8, other arithmetic, halves(): keep = pick(mine, at, axis) + pick(got, at, axis)  19.5 us
  transfers between devices with their start and end apart: 27, of which 11 were waited for; matrix products, arithmetic and copies ran while one was open for 32% of the time, Pallas kernels for 13%

profile of v1, /device:TPU:0, one launch (start us, length us, event | category | flops | bytes accessed | tf_op | source)
XLA Modules:
  0.0 518.3 jit_solution(11235099261326421273)
XLA Ops:
  31.0 4.4 convolution_convert_fusion.5.k_ref
  35.4 4.0 add_convert_fusion.6.v_ref
  39.4 4.0 add_convert_fusion.7.q_ref
  43.4 18.0 %attend_fwd.2 = (bf16[1024,768]{1,0:T(8,128)(2,1)}, f32[6,8,1024]{2,1,0:T(8,128)}) custom-call(bf16[1024,768]{1,0:T(8,128)(2,1)} %add_convert_fusion.7.q_ref, bf16[1024,768]{1,0:T(8,128)(2,1)} %convolution_convert_fusion.5.k_ref, bf16[1024,768]{1,0:T(8,128)(2,1)} %add_convert_fusion.6.v_ref, bf16[64,1024]{1,0:T(8,128)(2,1)} %fusion.16.oh_ref, ...), custom_call_target="tpu_custom_call" | custom-call | tf_op jit(solution)/shard_map/attend_fwd/pallas_call | solution.py:64
  61.4 3.5 fusion.37
  68.9 4.0 convolution_convert_fusion.4.k_ref
  72.9 4.0 add_convert_fusion.4.v_ref
  76.9 25.7 %attend_fwd.3 = (bf16[1024,768]{1,0:T(8,128)(2,1)}, f32[6,8,1024]{2,1,0:T(8,128)}) custom-call(bf16[1024,768]{1,0:T(8,128)(2,1)} %add_convert_fusion.5.q_ref, bf16[1024,768]{1,0:T(8,128)(2,1)} %convolution_convert_fusion.4.k_ref, bf16[1024,768]{1,0:T(8,128)(2,1)} %add_convert_fusion.4.v_ref, bf16[64,1024]{1,0:T(8,128)(2,1)} %fusion.16.oh_ref, ...), custom_call_target="tpu_custom_call" | custom-call | tf_op jit(solution)/shard_map/attend_fwd/pallas_call | solution.py:64
  102.7 3.7 fusion.38
  107.2 35.0 %multiply_convert_fusion = (bf16[1024,3072]{1,0:T(8,128)(2,1)S(1)}, f32[1024,3072]{1,0:T(8,128)}, f32[1024,3072]{1,0:T(8,128)}) fusion(f32[3072]{0:T(1024)S(1)} %copy-done.47, bf16[768,3072]{1,0:T(8,128)(2,1)S(1)} %bitcast.243, f32[1024,768]{1,0:T(8,128)S(1)} %get-tuple-element.128, f32[768]{0:T(1024)S(1)} %copy-done.53, f32[768]{0:T(1024)S(1)} %convert_element_type.249, ...), kind=kOutput, calls=%fused_computation.3 | convolution fusion | flops 5043388416 | bytes 39348224 | tf_op jit(solution)/shard_map/dot_general | solution.py:139
  142.2 5.5 %fusion.39 = (f32[1024]{0:T(1024)S(1)}, f32[1024,768]{1,0:T(8,128)S(1)}) fusion(f32[768]{0:T(1024)S(1)} %copy-done.54, bf16[1024,3072]{1,0:T(8,128)(2,1)S(1)} %get-tuple-element.67, bf16[3072,768]{1,0:T(8,128)(2,1)S(1)} %bitcast.241, f32[768]{0:T(1024)S(1)} %copy-done.53, f32[768]{0:T(1024)S(1)} %convert_element_type.249, f32[1024]{0:T(1024)S(1)} %fusion.20, ...), kind=kOutput, calls=%fused_computation.180 | convolution fusion | flops 4837342208 | bytes 17323008 | tf_op jit(solution)/shard_map/dot_general | solution.py:139
  148.3 3.5 fusion.9
  151.8 3.8 fusion.33
  157.7 7.0 %convolution_convert_fusion = bf16[3072,768]{1,0:T(8,128)(2,1)} fusion(bf16[1024,3072]{1,0:T(8,128)(2,1)S(1)} %get-tuple-element.67, bf16[1024,768]{1,0:T(8,128)(2,1)S(1)} %get-tuple-element.56), kind=kOutput, calls=%fused_computation.17 | convolution fusion | flops 4834197504 | bytes 12582912 | tf_op jit(solution)/shard_map/dot_general | solution.py:560
  164.6 18.9 %fusion.40 = (bf16[3072]{0:T(1024)(128)(2,1)}, bf16[1024,3072]{1,0:T(8,128)(2,1)}) fusion(f32[1024,3072]{1,0:T(8,128)} %get-tuple-element.68, bf16[1024,768]{1,0:T(8,128)(2,1)} %copy-done.21, bf16[3072,768]{1,0:T(8,128)(2,1)} %param.54, f32[1024,3072]{1,0:T(8,128)} %get-tuple-element.129, f32[3072]{0:T(1024)S(1)} %copy-done.47), kind=kOutput, calls=%fused_computation.181 | convolution fusion | flops 4882166784 | bytes 37767168 | tf_op jit(solution)/shard_map/dot_general | solution.py:564
  183.5 10.6 %convolution_convert_fusion.1 = bf16[768,3072]{1,0:T(8,128)(2,1)} fusion(bf16[1024,3072]{1,0:T(8,128)(2,1)} %get-tuple-element.135, f32[1024,768]{1,0:T(8,128)S(1)} %copy-done.7, f32[768]{0:T(1024)S(1)} %copy-done.53, f32[768]{0:T(1024)S(1)} %convert_element_type.249, f32[1024]{0:T(1024)S(1)} %fusion.20, f32[1024]{0:T(1024)S(1)} %broadcast_multiply_fusion.1), kind=kOutput, calls=%fused_computation.18 | convolution fusion | flops 4838129664 | bytes 14170112 | tf_op jit(solution)/shard_map/dot_general | solution.py:560
  194.1 9.0 %multiply_reduce_fusion = (bf16[768]{0:T(1024)(128)(2,1)}, f32[1024]{0:T(1024)S(1)}, bf16[768]{0:T(1024)(128)(2,1)}, f32[1024,768]{1,0:T(8,128)S(1)}) fusion(f32[1024,768]{1,0:T(8,128)S(1)} %copy-done.7, f32[1024]{0:T(1024)S(1)} %fusion.20, f32[1024]{0:T(1024)S(1)} %broadcast_multiply_fusion.1, f32[768]{0:T(1024)S(1)} %convert_element_type.249, ...), kind=kOutput, calls=%fused_computation.29 | convolution fusion | flops 4839699456 | bytes 20469760 | tf_op jit(solution)/shard_map/dot_general | solution.py:564
  211.9 34.9 %attend_bwd.2 = (bf16[1024,768]{1,0:T(8,128)(2,1)}, bf16[1024,768]{1,0:T(8,128)(2,1)}, bf16[1024,768]{1,0:T(8,128)(2,1)}) custom-call(bf16[1024,768]{1,0:T(8,128)(2,1)} %add_convert_fusion.5.q_ref, bf16[1024,768]{1,0:T(8,128)(2,1)} %convolution_convert_fusion.4.k_ref, bf16[1024,768]{1,0:T(8,128)(2,1)} %add_convert_fusion.4.v_ref, ...), custom_call_target="tpu_custom_call" | custom-call | tf_op jit(solution)/shard_map/attend_bwd/pallas_call | solution.py:129
  276.1 24.5 %attend_bwd.3 = (bf16[1024,768]{1,0:T(8,128)(2,1)}, bf16[1024,768]{1,0:T(8,128)(2,1)}, bf16[1024,768]{1,0:T(8,128)(2,1)}) custom-call(bf16[1024,768]{1,0:T(8,128)(2,1)} %add_convert_fusion.7.q_ref, bf16[1024,768]{1,0:T(8,128)(2,1)} %convolution_convert_fusion.5.k_ref, bf16[1024,768]{1,0:T(8,128)(2,1)} %add_convert_fusion.6.v_ref, ...), custom_call_target="tpu_custom_call" | custom-call | tf_op jit(solution)/shard_map/attend_bwd/pallas_call | solution.py:129
  336.0 3.4 bitcast_add_fusion.5
  341.1 3.4 bitcast_add_fusion.7
  347.1 3.4 bitcast_add_fusion.3
  351.6 3.6 bitcast_add_fusion.1
  359.9 8.8 %collective-permute-done.23 = bf16[2,2,192,768]{3,2,1,0:T(8,128)(2,1)} collective-permute-done((bf16[2,2,192,768]{3,2,1,0:T(8,128)(2,1)}, bf16[2,2,192,768]{3,2,1,0:T(8,128)(2,1)}, u32[]{:S(2)}, u32[]{:S(2)}) %collective-permute-start.23) | collective-permute-done | bytes 1179680 | tf_op jit(solution)/shard_map/ppermute | solution.py:513
  373.1 20.9 %collective-permute-done.18 = bf16[2,2,48,3072]{3,2,1,0:T(8,128)(2,1)} collective-permute-done((bf16[2,2,48,3072]{3,2,1,0:T(8,128)(2,1)}, bf16[2,2,48,3072]{3,2,1,0:T(8,128)(2,1)}, u32[]{:S(2)}, u32[]{:S(2)}) %collective-permute-start.18) | collective-permute-done | bytes 1179680 | tf_op jit(solution)/shard_map/ppermute | solution.py:513
  401.8 17.5 %collective-permute-done.13 = bf16[2,2,192,768]{3,2,1,0:T(8,128)(2,1)} collective-permute-done((bf16[2,2,192,768]{3,2,1,0:T(8,128)(2,1)}, bf16[2,2,192,768]{3,2,1,0:T(8,128)(2,1)}, u32[]{:S(2)}, u32[]{:S(2)}) %collective-permute-start.13) | collective-permute-done | bytes 1179680 | tf_op jit(solution)/shard_map/ppermute | solution.py:513
  422.3 23.4 %collective-permute-done.8 = bf16[2,2,208,768]{3,2,1,0:T(8,128)(2,1)} collective-permute-done((bf16[2,2,208,768]{3,2,1,0:T(8,128)(2,1)}, bf16[2,2,208,768]{3,2,1,0:T(8,128)(2,1)}, u32[]{:S(2)}, u32[]{:S(2)}) %collective-permute-start.8) | collective-permute-done | bytes 1277984 | tf_op jit(solution)/shard_map/ppermute | solution.py:513
  454.8 15.4 %collective-permute-done.25 = bf16[192,768]{1,0:T(8,128)(2,1)S(1)} collective-permute-done((bf16[192,768]{1,0:T(8,128)(2,1)S(1)}, bf16[192,768]{1,0:T(8,128)(2,1)S(1)}, u32[]{:S(2)}, u32[]{:S(2)}) %collective-permute-start.25) | collective-permute-done | bytes 294944 | tf_op jit(solution)/shard_map/ppermute | solution.py:513
  471.8 13.4 %collective-permute-done.20 = bf16[48,3072]{1,0:T(8,128)(2,1)S(1)} collective-permute-done((bf16[48,3072]{1,0:T(8,128)(2,1)S(1)}, bf16[48,3072]{1,0:T(8,128)(2,1)S(1)}, u32[]{:S(2)}, u32[]{:S(2)}) %collective-permute-start.20) | collective-permute-done | bytes 294944 | tf_op jit(solution)/shard_map/ppermute | solution.py:513
  494.3 4.0 collective-permute-done.16
  498.4 7.9 %collective-permute-done.10 = bf16[208,768]{1,0:T(8,128)(2,1)S(1)} collective-permute-done((bf16[208,768]{1,0:T(8,128)(2,1)S(1)}, bf16[208,768]{1,0:T(8,128)(2,1)S(1)}, u32[]{:S(2)}, u32[]{:S(2)}) %collective-permute-start.10) | collective-permute-done | bytes 319520 | tf_op jit(solution)/shard_map/ppermute | solution.py:513
  508.6 7.3 %collective-permute-done.11 = bf16[208,768]{1,0:T(8,128)(2,1)S(1)} collective-permute-done((bf16[208,768]{1,0:T(8,128)(2,1)S(1)}, bf16[208,768]{1,0:T(8,128)(2,1)S(1)}, u32[]{:S(2)}, u32[]{:S(2)}) %collective-permute-start.11) | collective-permute-done | bytes 319520 | tf_op jit(solution)/shard_map/ppermute | solution.py:513
  (370 shorter events, 160.1 us)
Async XLA Ops:
  0.7 65.4 %copy-start = (bf16[768,768]{1,0:T(8,128)(2,1)S(1)}, bf16[768,768]{1,0:T(8,128)(2,1)}, u32[]{:S(2)}) copy-start(bf16[768,768]{1,0:T(8,128)(2,1)} %param.43) | copy-start | bytes 3538948
  2.2 25.5 %collective-permute-start.1 = (s32[512,2]{0,1:T(2,128)}, s32[512,2]{0,1:T(2,128)}, u32[]{:S(2)}, u32[]{:S(2)}) collective-permute-start(s32[512,2]{0,1:T(2,128)} %bitcast.203), channel_id=1, source_target_pairs={{0,1},{1,0},{2,3},{3,2},{4,5},{5,4},{6,7},{7,6},{8,9},{9,8},{10,11... | collective-permute-start | bytes 12296 | tf_op jit(solution)/shard_map/ppermute | solution.py:513
  7.5 53.9 %copy-start.31 = (bf16[512,768]{1,0:T(8,128)(2,1)}, bf16[512,768]{1,0:T(8,128)(2,1)S(1)}, u32[]{:S(2)}) copy-start(bf16[512,768]{1,0:T(8,128)(2,1)S(1)} %get-tuple-element.96) | copy-start | bytes 2359300
  7.5 23.4 %collective-permute-start = (bf16[512,768]{1,0:T(8,128)(2,1)}, bf16[512,768]{1,0:T(8,128)(2,1)}, u32[]{:S(2)}, u32[]{:S(2)}) collective-permute-start(bf16[512,768]{1,0:T(8,128)(2,1)} %get-tuple-element.97), channel_id=1, source_target_pairs={{0,1},{1,0},{2,3},{3,2},{4,5},{5,4},{6,7},{7,6},{8,9},{9,8},{10,11... | collective-permute-start | bytes 2359304 | tf_op jit(solution)/shard_map/ppermute | solution.py:513
  9.0 59.9 %collective-permute-start.2 = (bf16[512,768]{1,0:T(8,128)(2,1)}, bf16[512,768]{1,0:T(8,128)(2,1)}, u32[]{:S(2)}, u32[]{:S(2)}) collective-permute-start(bf16[512,768]{1,0:T(8,128)(2,1)} %get-tuple-element.95), channel_id=1, source_target_pairs={{0,1},{1,0},{2,3},{3,2},{4,5},{5,4},{6,7},{7,6},{8,9},{9,8},{10,11... | collective-permute-start | bytes 2359304 | tf_op jit(solution)/shard_map/ppermute | solution.py:513
  11.9 136.3 %collective-permute-start.4 = (bf16[512,768]{1,0:T(8,128)(2,1)}, bf16[512,768]{1,0:T(8,128)(2,1)S(1)}, u32[]{:S(2)}, u32[]{:S(2)}) collective-permute-start(bf16[512,768]{1,0:T(8,128)(2,1)} %get-tuple-element.90), channel_id=1, source_target_pairs={{0,1},{1,0},{2,3},{3,2},{4,5},{5,4},{6,7},{7,6},{8,9},{9,8},{10,11... | collective-permute-start | bytes 2359304 | tf_op jit(solution)/shard_map/ppermute | solution.py:513
  16.7 85.9 %copy-start.43 = (f32[768]{0:T(1024)}, f32[768]{0:T(1024)S(1)}, u32[]{:S(2)}) copy-start(f32[768]{0:T(1024)S(1)} %convert_element_type.239) | copy-start | bytes 9220
  102.7 39.5 %slice-start.10 = ((s8[4718592]{0:T(1024)(128)(4,1)}), s8[4194304]{0:T(1024)(128)(4,1)S(1)}, s32[]{:S(2)}) async-start(s8[4718592]{0:T(1024)(128)(4,1)} %bitcast.240), calls=%async_computation.10 | async-start | bytes 8388608
  263.4 71.8 %collective-permute-start.22 = (bf16[2,2,2,192,768]{4,3,2,1,0:T(8,128)(2,1)}, bf16[2,2,2,192,768]{4,3,2,1,0:T(8,128)(2,1)}, u32[]{:S(2)}, u32[]{:S(2)}) collective-permute-start(bf16[2,2,2,192,768]{4,3,2,1,0:T(8,128)(2,1)} %dynamic-slice_bitcast_fusion.1), channel_id=1, source_target_pairs={{0,2},{2,0},{4,6},{6,4},{8,10},{10,8},{12,14},{14,12},{16,18},{18,... | collective-permute-start | bytes 7077896 | tf_op jit(solution)/shard_map/ppermute | solution.py:513
  265.2 75.9 %collective-permute-start.17 = (bf16[2,2,2,48,3072]{4,3,2,1,0:T(8,128)(2,1)}, bf16[2,2,2,48,3072]{4,3,2,1,0:T(8,128)(2,1)}, u32[]{:S(2)}, u32[]{:S(2)}) collective-permute-start(bf16[2,2,2,48,3072]{4,3,2,1,0:T(8,128)(2,1)} %dynamic-slice_bitcast_fusion.2), channel_id=1, source_target_pairs={{0,2},{2,0},{4,6},{6,4},{8,10},{10,8},{12,14},{14,12},{16,18},{18,... | collective-permute-start | bytes 7077896 | tf_op jit(solution)/shard_map/ppermute | solution.py:513
  276.1 71.0 %collective-permute-start.12 = (bf16[2,2,2,192,768]{4,3,2,1,0:T(8,128)(2,1)}, bf16[2,2,2,192,768]{4,3,2,1,0:T(8,128)(2,1)}, u32[]{:S(2)}, u32[]{:S(2)}) collective-permute-start(bf16[2,2,2,192,768]{4,3,2,1,0:T(8,128)(2,1)} %dynamic-slice_bitcast_fusion.3), channel_id=1, source_target_pairs={{0,2},{2,0},{4,6},{6,4},{8,10},{10,8},{12,14},{14,12},{16,18},{18,... | collective-permute-start | bytes 7077896 | tf_op jit(solution)/shard_map/ppermute | solution.py:513
  326.7 24.9 %collective-permute-start.7 = (bf16[2,2,2,208,768]{4,3,2,1,0:T(8,128)(2,1)S(1)}, bf16[2,2,2,208,768]{4,3,2,1,0:T(8,128)(2,1)S(1)}, u32[]{:S(2)}, u32[]{:S(2)}) collective-permute-start(bf16[2,2,2,208,768]{4,3,2,1,0:T(8,128)(2,1)S(1)} %dynamic-slice_bitcast_fusion), channel_id=1, source_target_pairs={{0,2},{2,0},{4,6},{6,4},{8,10},{10,8},{12,14},{14,12},{16,18},{18,... | collective-permute-start | bytes 7667720 | tf_op jit(solution)/shard_map/ppermute | solution.py:513
  330.3 27.0 %collective-permute-start.6 = (bf16[512,768]{1,0:T(8,128)(2,1)S(1)}, bf16[512,768]{1,0:T(8,128)(2,1)S(1)}, u32[]{:S(2)}, u32[]{:S(2)}) collective-permute-start(bf16[512,768]{1,0:T(8,128)(2,1)S(1)} %get-tuple-element.87), channel_id=1, source_target_pairs={{0,1},{1,0},{2,3},{3,2},{4,5},{5,4},{6,7},{7,6},{8,9},{9,8},{10,11... | collective-permute-start | bytes 2359304 | tf_op jit(solution)/shard_map/ppermute | solution.py:513
  339.4 29.4 %collective-permute-start.23 = (bf16[2,2,192,768]{3,2,1,0:T(8,128)(2,1)}, bf16[2,2,192,768]{3,2,1,0:T(8,128)(2,1)}, u32[]{:S(2)}, u32[]{:S(2)}) collective-permute-start(bf16[2,2,192,768]{3,2,1,0:T(8,128)(2,1)} %get-tuple-element.72), channel_id=1, source_target_pairs={{0,4},{2,6},{4,0},{6,2},{8,12},{10,14},{12,8},{14,10},{16,20},{18,... | collective-permute-start | bytes 3538952 | tf_op jit(solution)/shard_map/ppermute | solution.py:513
  344.5 49.5 %collective-permute-start.18 = (bf16[2,2,48,3072]{3,2,1,0:T(8,128)(2,1)}, bf16[2,2,48,3072]{3,2,1,0:T(8,128)(2,1)}, u32[]{:S(2)}, u32[]{:S(2)}) collective-permute-start(bf16[2,2,48,3072]{3,2,1,0:T(8,128)(2,1)} %get-tuple-element.74), channel_id=1, source_target_pairs={{0,4},{2,6},{4,0},{6,2},{8,12},{10,14},{12,8},{14,10},{16,20},{18,... | collective-permute-start | bytes 3538952 | tf_op jit(solution)/shard_map/ppermute | solution.py:513
  350.5 68.8 %collective-permute-start.13 = (bf16[2,2,192,768]{3,2,1,0:T(8,128)(2,1)}, bf16[2,2,192,768]{3,2,1,0:T(8,128)(2,1)}, u32[]{:S(2)}, u32[]{:S(2)}) collective-permute-start(bf16[2,2,192,768]{3,2,1,0:T(8,128)(2,1)} %get-tuple-element.76), channel_id=1, source_target_pairs={{0,4},{2,6},{4,0},{6,2},{8,12},{10,14},{12,8},{14,10},{16,20},{18,... | collective-permute-start | bytes 3538952 | tf_op jit(solution)/shard_map/ppermute | solution.py:513
  355.2 90.4 %collective-permute-start.8 = (bf16[2,2,208,768]{3,2,1,0:T(8,128)(2,1)}, bf16[2,2,208,768]{3,2,1,0:T(8,128)(2,1)}, u32[]{:S(2)}, u32[]{:S(2)}) collective-permute-start(bf16[2,2,208,768]{3,2,1,0:T(8,128)(2,1)} %get-tuple-element.70), channel_id=1, source_target_pairs={{0,4},{2,6},{4,0},{6,2},{8,12},{10,14},{12,8},{14,10},{16,20},{18,... | collective-permute-start | bytes 3833864 | tf_op jit(solution)/shard_map/ppermute | solution.py:513
  358.3 38.7 %collective-permute-start.5 = (bf16[512,768]{1,0:T(8,128)(2,1)}, bf16[512,768]{1,0:T(8,128)(2,1)}, u32[]{:S(2)}, u32[]{:S(2)}) collective-permute-start(bf16[512,768]{1,0:T(8,128)(2,1)} %get-tuple-element.89), channel_id=1, source_target_pairs={{0,1},{1,0},{2,3},{3,2},{4,5},{5,4},{6,7},{7,6},{8,9},{9,8},{10,11... | collective-permute-start | bytes 2359304 | tf_op jit(solution)/shard_map/ppermute | solution.py:513
  368.7 31.7 %collective-permute-start.3 = (bf16[512,768]{1,0:T(8,128)(2,1)S(1)}, bf16[512,768]{1,0:T(8,128)(2,1)S(1)}, u32[]{:S(2)}, u32[]{:S(2)}) collective-permute-start(bf16[512,768]{1,0:T(8,128)(2,1)S(1)} %get-tuple-element.93), channel_id=1, source_target_pairs={{0,1},{1,0},{2,3},{3,2},{4,5},{5,4},{6,7},{7,6},{8,9},{9,8},{10,11... | collective-permute-start | bytes 2359304 | tf_op jit(solution)/shard_map/ppermute | solution.py:513
  394.0 55.0 %collective-permute-start.24 = (bf16[2,192,768]{2,1,0:T(8,128)(2,1)S(1)}, bf16[2,192,768]{2,1,0:T(8,128)(2,1)S(1)}, u32[]{:S(2)}, u32[]{:S(2)}) collective-permute-start(bf16[2,192,768]{2,1,0:T(8,128)(2,1)S(1)} %get-tuple-element.81), channel_id=1, source_target_pairs={{0,8},{2,10},{4,12},{6,14},{8,0},{10,2},{12,4},{14,6},{16,24},{18,... | collective-permute-start | bytes 1769480 | tf_op jit(solution)/shard_map/ppermute | solution.py:513
  396.9 54.7 %collective-permute-start.19 = (bf16[2,48,3072]{2,1,0:T(8,128)(2,1)S(1)}, bf16[2,48,3072]{2,1,0:T(8,128)(2,1)S(1)}, u32[]{:S(2)}, u32[]{:S(2)}) collective-permute-start(bf16[2,48,3072]{2,1,0:T(8,128)(2,1)S(1)} %get-tuple-element.83), channel_id=1, source_target_pairs={{0,8},{2,10},{4,12},{6,14},{8,0},{10,2},{12,4},{14,6},{16,24},{18,... | collective-permute-start | bytes 1769480 | tf_op jit(solution)/shard_map/ppermute | solution.py:513
  400.4 45.2 %copy-start.14 = (bf16[2,2,208,768]{3,2,1,0:T(8,128)(2,1)S(1)}, bf16[2,2,208,768]{3,2,1,0:T(8,128)(2,1)}, u32[]{:S(2)}) copy-start(bf16[2,2,208,768]{3,2,1,0:T(8,128)(2,1)} %get-tuple-element.69) | copy-start | bytes 3833860
  420.7 31.4 %collective-permute-start.14 = (bf16[2,192,768]{2,1,0:T(8,128)(2,1)S(1)}, bf16[2,192,768]{2,1,0:T(8,128)(2,1)S(1)}, u32[]{:S(2)}, u32[]{:S(2)}) collective-permute-start(bf16[2,192,768]{2,1,0:T(8,128)(2,1)S(1)} %get-tuple-element.85), channel_id=1, source_target_pairs={{0,8},{2,10},{4,12},{6,14},{8,0},{10,2},{12,4},{14,6},{16,24},{18,... | collective-permute-start | bytes 1769480 | tf_op jit(solution)/shard_map/ppermute | solution.py:513
  447.1 44.2 %collective-permute-start.9 = (bf16[2,208,768]{2,1,0:T(8,128)(2,1)S(1)}, bf16[2,208,768]{2,1,0:T(8,128)(2,1)S(1)}, u32[]{:S(2)}, u32[]{:S(2)}) collective-permute-start(bf16[2,208,768]{2,1,0:T(8,128)(2,1)S(1)} %get-tuple-element.79), channel_id=1, source_target_pairs={{0,8},{2,10},{4,12},{6,14},{8,0},{10,2},{12,4},{14,6},{16,24},{18,... | collective-permute-start | bytes 1916936 | tf_op jit(solution)/shard_map/ppermute | solution.py:513
  449.0 21.2 %collective-permute-start.25 = (bf16[192,768]{1,0:T(8,128)(2,1)S(1)}, bf16[192,768]{1,0:T(8,128)(2,1)S(1)}, u32[]{:S(2)}, u32[]{:S(2)}) collective-permute-start(bf16[192,768]{1,0:T(8,128)(2,1)S(1)} %fusion.13), channel_id=1, source_target_pairs={{0,16},{2,18},{4,20},{6,22},{8,24},{10,26},{12,28},{14,30},{16,0},... | collective-permute-start | bytes 884744 | tf_op jit(solution)/shard_map/ppermute | solution.py:513
  451.7 33.5 %collective-permute-start.20 = (bf16[48,3072]{1,0:T(8,128)(2,1)S(1)}, bf16[48,3072]{1,0:T(8,128)(2,1)S(1)}, u32[]{:S(2)}, u32[]{:S(2)}) collective-permute-start(bf16[48,3072]{1,0:T(8,128)(2,1)S(1)} %fusion.14), channel_id=1, source_target_pairs={{0,16},{2,18},{4,20},{6,22},{8,24},{10,26},{12,28},{14,30},{16,0},... | collective-permute-start | bytes 884744 | tf_op jit(solution)/shard_map/ppermute | solution.py:513
  452.2 37.5 %collective-permute-start.15 = (bf16[192,768]{1,0:T(8,128)(2,1)S(1)}, bf16[192,768]{1,0:T(8,128)(2,1)S(1)}, u32[]{:S(2)}, u32[]{:S(2)}) collective-permute-start(bf16[192,768]{1,0:T(8,128)(2,1)S(1)} %fusion.15), channel_id=1, source_target_pairs={{0,16},{2,18},{4,20},{6,22},{8,24},{10,26},{12,28},{14,30},{16,0},... | collective-permute-start | bytes 884744 | tf_op jit(solution)/shard_map/ppermute | solution.py:513
  470.2 37.5 %collective-permute-start.26 = (bf16[192,768]{1,0:T(8,128)(2,1)S(1)}, bf16[192,768]{1,0:T(8,128)(2,1)S(1)}, u32[]{:S(2)}, u32[]{:S(2)}) collective-permute-start(bf16[192,768]{1,0:T(8,128)(2,1)S(1)} %bitcast_add_fusion.12), channel_id=1, source_target_pairs={{0,1},{1,0},{2,3},{3,2},{4,5},{5,4},{6,7},{7,6},{8,9},{9,8},{10,11... | collective-permute-start | bytes 884744 | tf_op jit(solution)/shard_map/ppermute | solution.py:513
  485.3 8.2 %collective-permute-start.21 = (bf16[48,3072]{1,0:T(8,128)(2,1)S(1)}, bf16[48,3072]{1,0:T(8,128)(2,1)S(1)}, u32[]{:S(2)}, u32[]{:S(2)}) collective-permute-start(bf16[48,3072]{1,0:T(8,128)(2,1)S(1)} %bitcast_add_fusion.15), channel_id=1, source_target_pairs={{0,1},{1,0},{2,3},{3,2},{4,5},{5,4},{6,7},{7,6},{8,9},{9,8},{10,11... | collective-permute-start | bytes 884744 | tf_op jit(solution)/shard_map/ppermute | solution.py:513
  489.7 8.7 %collective-permute-start.16 = (bf16[192,768]{1,0:T(8,128)(2,1)S(1)}, bf16[192,768]{1,0:T(8,128)(2,1)S(1)}, u32[]{:S(2)}, u32[]{:S(2)}) collective-permute-start(bf16[192,768]{1,0:T(8,128)(2,1)S(1)} %bitcast_add_fusion.18), channel_id=1, source_target_pairs={{0,1},{1,0},{2,3},{3,2},{4,5},{5,4},{6,7},{7,6},{8,9},{9,8},{10,11... | collective-permute-start | bytes 884744 | tf_op jit(solution)/shard_map/ppermute | solution.py:513
  491.3 15.0 %collective-permute-start.10 = (bf16[208,768]{1,0:T(8,128)(2,1)S(1)}, bf16[208,768]{1,0:T(8,128)(2,1)S(1)}, u32[]{:S(2)}, u32[]{:S(2)}) collective-permute-start(bf16[208,768]{1,0:T(8,128)(2,1)S(1)} %fusion.12), channel_id=1, source_target_pairs={{0,16},{2,18},{4,20},{6,22},{8,24},{10,26},{12,28},{14,30},{16,0},... | collective-permute-start | bytes 958472 | tf_op jit(solution)/shard_map/ppermute | solution.py:513
  506.4 9.5 %collective-permute-start.11 = (bf16[208,768]{1,0:T(8,128)(2,1)S(1)}, bf16[208,768]{1,0:T(8,128)(2,1)S(1)}, u32[]{:S(2)}, u32[]{:S(2)}) collective-permute-start(bf16[208,768]{1,0:T(8,128)(2,1)S(1)} %bitcast_add_fusion.9), channel_id=1, source_target_pairs={{0,1},{1,0},{2,3},{3,2},{4,5},{5,4},{6,7},{7,6},{8,9},{9,8},{10,11... | collective-permute-start | bytes 958472 | tf_op jit(solution)/shard_map/ppermute | solution.py:513
  (92 other events, 932.1 us)

commit v2 on v0

--- a/solution.py
+++ b/solution.py
@@ -1,11 +1,133 @@
+import functools
 import math
 
 import jax
 import jax.numpy as jnp
 from jax import lax
+from jax.experimental import pallas as pl
+from jax.experimental.pallas import tpu as pltpu
 from jax.sharding import PartitionSpec as P
 
 HEADS = 12
+BF=jnp.bfloat16; F32=jnp.float32
+BIG=-1e30
+def dot(a,b): return jnp.dot(a,b,preferred_element_type=F32)
+
+def lane_low(shape): return lax.broadcasted_iota(jnp.int32, shape, 1) < 64
+
+def masks(seg_q, seg_k):
+    T=seg_q.shape[0]; K=seg_k.shape[0]
+    r=jnp.arange(64)[:,None]
+    oh=((r==seg_q[None,:])).astype(BF)
+    c=jnp.arange(128)[None,:]%64
+    mk=jnp.where(c<4, jnp.where(c==seg_k[:,None],0.0,BIG), jnp.where(c<7,-1.0,0.0)).astype(BF)
+    return oh,mk
+
+def attend_pair(q,k,v,oh,mk,put_total,bq,causal):
+    T=q.shape[0]; K=k.shape[0]
+    low=lane_low((K,128))
+    qT=(q*BF(0.125)).T
+    vT=v.T
+    ones=jnp.ones((16,K),BF)
+    if causal:
+        dm=lax.broadcasted_iota(jnp.int32,(bq,bq),0)<=lax.broadcasted_iota(jnp.int32,(bq,bq),1)
+    kas=[jnp.where(low,k,mk),jnp.where(low,mk,k)]
+    vas=[jnp.concatenate([vT[64*h:64*h+64],ones],0) for h in (0,1)]
+    qas=[jnp.concatenate([qT[:64],oh],0),jnp.concatenate([oh,qT[64:]],0)]
+    def scores(i,h):
+        qa=qas[h][:,i*bq:(i+1)*bq]
+        if not causal: return [dot(kas[h],qa)]
+        here=jnp.where(dm,dot(kas[h][i*bq:(i+1)*bq],qa),BIG)
+        return [dot(kas[h][:i*bq],qa),here] if i else [here]
+    def weigh(s):
+        m=functools.reduce(jnp.maximum,[jnp.max(x,axis=0,keepdims=True) for x in s])
+        return m,[jnp.exp(x-m).astype(BF) for x in s]
+    def mix(i,h,m,ps):
+        o=None; at=0
+        for p in ps:
+            t=dot(vas[h][:,at:at+p.shape[0]],p); at+=p.shape[0]
+            o=t if o is None else o+t
+        l=o[64:65]
+        put_total(h,i,m+jnp.log(l))
+        return o[:64]/l
+    units=[(i,h) for i in range(T//bq) for h in (0,1)]
+    os=[]
+    s=scores(*units[0]); late=None
+    for n,u in enumerate(units):
+        coming=scores(*units[n+1]) if n+1<len(units) else None
+        m,ps=weigh(s)
+        if late is not None: os.append(mix(*late))
+        late=(*u,m,ps)
+        s=coming
+    os.append(mix(*late))
+    return [jnp.concatenate(os[2*i:2*i+2],0).T.astype(BF) for i in range(T//bq)]
+
+def split3(x):
+    a=x.astype(BF); r=x-a.astype(F32); b=r.astype(BF); c=(r-b.astype(F32)).astype(BF)
+    return a,b,c
+
+def attend_pair_back(q,k,v,do,o,totals,oh,mk,acc_ref,put,bk,causal):
+    T=q.shape[0]; K=k.shape[0]
+    low=lane_low((K,128))
+    q=q*BF(0.125)
+    qT=q.T; doT=do.T
+    kT=k.T
+    prodT=(do.astype(F32)*o.astype(F32)).T
+    rowi=lax.broadcasted_iota(jnp.int32,(64,T),0)
+    one=jnp.full((K,128),-1.0,BF)
+    if causal:
+        dm=lax.broadcasted_iota(jnp.int32,(bk,bk),0)<=lax.broadcasted_iota(jnp.int32,(bk,bk),1)
+    qas=[];das=[]
+    for h in (0,1):
+        a,b,c=split3(totals[h])
+        ohl=jnp.where(rowi==4,a,jnp.where(rowi==5,b,jnp.where(rowi==6,c,oh)))
+        D=jnp.sum(prodT[64*h:64*h+64],axis=0,keepdims=True)
+        a,b,c=split3(D)
+        z=jnp.zeros((64,T),BF)
+        dd=jnp.where(rowi==0,a,jnp.where(rowi==1,b,jnp.where(rowi==2,c,z)))
+        if h==0:
+            qas.append(jnp.concatenate([qT[:64],ohl],0)); das.append(jnp.concatenate([doT[:64],dd],0))
+        else:
+            qas.append(jnp.concatenate([ohl,qT[64:]],0)); das.append(jnp.concatenate([dd,doT[64:]],0))
+    kas=[jnp.where(low,k,mk),jnp.where(low,mk,k)]
+    vas=[jnp.where(low,v,one),jnp.where(low,one,v)]
+    for j in range(K//bk):
+        dks=[];dvs=[]
+        q0=j*bk if causal else 0
+        ks=slice(j*bk,(j+1)*bk)
+        for h in (0,1):
+            s=dot(kas[h][ks],qas[h][:,q0:])
+            if causal:
+                sd=jnp.where(dm,s[:,:bk],BIG)
+                s=jnp.concatenate([sd,s[:,bk:]],1) if q0+bk<T else sd
+            p=jnp.exp(s)
+            dp=dot(vas[h][ks],das[h][:,q0:])
+            ds=(p*dp).astype(BF)
+            dvs.append(dot(p.astype(BF),do[q0:]))
+            dks.append(dot(ds,q[q0:]))
+            dqt=dot(kT[64*h:64*h+64,ks],ds)
+            if j==0: acc_ref[64*h:64*h+64,:]=dqt
+            else: acc_ref[64*h:64*h+64,q0:]+=dqt
+        lw=low[:bk]
+        put("k",ks,jnp.where(lw,dks[0],dks[1]).astype(BF))
+        put("v",ks,jnp.where(lw,dvs[0],dvs[1]).astype(BF))
+    put("q",slice(0,T),(acc_ref[...]*0.125).T.astype(BF))
+
+def bwd_kernel(spot_ref,q_ref,k_ref,v_ref,do_ref,o_ref,l_ref,oh_ref,mk_ref,dq_ref,dk_ref,dv_ref,acc_ref,*,bk,causal):
+    out={"q":dq_ref,"k":dk_ref,"v":dv_ref}
+    def put(name,rows,block): out[name][rows,:]=block
+    attend_pair_back(q_ref[...],k_ref[...],v_ref[...],do_ref[...],o_ref[...],[l_ref[0,h:h+1,:] for h in (0,1)],
+                     oh_ref[...],mk_ref[...],acc_ref,put,bk,causal)
+
+def attend_bwd(order,spots,q,k,v,do,o,l,oh,mk,causal,bk=256,p0=0,np_=None,moves=()):
+    T,D=q.shape; K=k.shape[0]; n=np_ or D//128
+    pin=lambda r:pl.BlockSpec((r,128),lambda p,c:(0,p+p0))
+    po=lambda r:pl.BlockSpec((r,128),lambda p,c:(0,p))
+    return order.call(functools.partial(bwd_kernel,bk=bk,causal=causal),spots,q,k,v,do,o,l,oh,mk,scalars=1,name="attend_bwd",us=4*n,grid=(n,),moves=moves,
+        in_specs=[pin(T),pin(K),pin(K),pin(T),pin(T),pl.BlockSpec((1,8,T),lambda p,c:(p+p0,0,0)),pl.BlockSpec((64,T),lambda p,c:(0,0)),pl.BlockSpec((K,128),lambda p,c:(0,0))],
+        out_specs=[po(T),po(K),po(K)],
+        out_shape=[jax.ShapeDtypeStruct((T,128*n),BF),jax.ShapeDtypeStruct((K,128*n),BF),jax.ShapeDtypeStruct((K,128*n),BF)],
+        scratch_shapes=[pltpu.VMEM((128,T),F32)])
 
 
 def project(values, weight):
@@ -90,7 +212,7 @@
     return (merge_heads(query_grads), merge_heads(key_terms), merge_heads(value_terms))
 
 
-def on_device(
+def split_rows(
     hidden_in,
     memory,
     tgt_segment,
@@ -382,6 +504,914 @@
     return (hidden_out, hidden_grad, memory_grad) + tuple(finished)
 
 
+def nt(a, b):
+    return lax.dot_general(a, b, (((1,), (1,)), ((), ())), preferred_element_type=F32)
+
+
+def tn(a, b):
+    return lax.dot_general(a, b, (((0,), (0,)), ((), ())), preferred_element_type=F32)
+
+
+def mean(v):
+    return jnp.mean(v, axis=-1, keepdims=True)
+
+
+def norm_stats(v):
+    center = v - mean(v)
+    r = lax.rsqrt(mean(center * center) + 1e-05)
+    return center * r, r
+
+
+def norm_back(e, n, r, gain):
+    u = e * gain
+    return r * (u - mean(u) - n * mean(u * n))
+
+
+def sums(v):
+    return jnp.sum(v, axis=0, keepdims=True)
+
+
+TAIL = (0.24251982196758853, 0.24429374300098905, 0.2054730204591465, 0.24507896666845616,
+        -0.08230106829392796, 0.3798837300580386, -0.30809352249830146, 0.07314529579847638)
+
+
+def gelu_pair(x):
+    d = 1.0 + (0.43 * math.sqrt(0.5)) * jnp.abs(x)
+    t = pl.reciprocal(d, approx=True)
+    t = t * (2.0 - d * t)
+    tail = 0.5 * TAIL[-1]
+    for c in TAIL[-2::-1]:
+        tail = tail * t + 0.5 * c
+    bell = jnp.exp(-0.5 * x * x)
+    tail = tail * t * bell
+    phi = jnp.where(x >= 0, 1.0 - tail, tail)
+    return x * phi, phi + x * bell * (1.0 / math.sqrt(2.0 * math.pi))
+
+
+def full(shape):
+    return pl.BlockSpec(shape, lambda *_: (0,) * len(shape), pipeline_mode=pl.Buffered(1))
+
+
+def still(shape):
+    return pl.BlockSpec(shape, lambda *_: (0,) * len(shape))
+
+
+def rows_of(bt, width):
+    return pl.BlockSpec((bt, width), lambda i: (i, 0))
+
+
+class Order:
+    def __init__(self):
+        self.last = []
+
+    def call(self, kernel, *args, name, us, grid, in_specs, out_specs, out_shape, scalars=0, scratch_shapes=(), moves=()):
+        at, after, n, n_out = len(args), len(self.last), len(moves), len(out_specs)
+        flat = [array for pair in moves for array in pair]
+        hbm = pl.BlockSpec(memory_space=pl.ANY)
+
+        def run(*refs):
+            outs = at + 2 * n + after
+            plain = refs[:at] + refs[outs : outs + n_out]
+            if not n:
+                return kernel(*plain, *refs[outs + n_out :])
+            s = refs[0][4]
+            buffer, sem = refs[-2:]
+            reads, writes = [], []
+            for i in range(n):
+                target = refs[outs + n_out + i]
+                for j, place in enumerate((s, 1 - s)):
+                    slot = 2 * i + j
+                    reads.append(pltpu.make_async_copy(refs[at + slot], buffer.at[slot], sem.at[0, slot]))
+                    writes.append(pltpu.make_async_copy(buffer.at[slot], target.at[place], sem.at[1, slot]))
+
+            @pl.when(pl.program_id(0) == 0)
+            def _():
+                for c in reads:
+                    c.start()
+
+            @pl.when(pl.program_id(0) == 1)
+            def _():
+                for r, w in zip(reads, writes):
+                    r.wait()
+                    w.start()
+
+            kernel(*plain, *refs[outs + n_out + n : -2])
+
+            @pl.when(pl.program_id(0) == grid[0] - 1)
+            def _():
+                for c in writes:
+                    c.wait()
+
+        more = [pltpu.VMEM((2 * n, *flat[0].shape), BF), pltpu.SemaphoreType.DMA((2, 2 * n))] if n else []
+        out = pl.pallas_call(
+            run, name=name, out_shape=list(out_shape) + [shaped(2, *pair[0].shape) for pair in moves],
+            grid_spec=pltpu.PrefetchScalarGridSpec(
+                num_scalar_prefetch=scalars, grid=grid, in_specs=list(in_specs) + [hbm] * (2 * n + after),
+                out_specs=list(out_specs) + [hbm] * n, scratch_shapes=list(scratch_shapes) + more),
+            cost_estimate=pl.CostEstimate(flops=0, bytes_accessed=int(us * 7.2e6), transcendentals=0),
+            compiler_params=pltpu.CompilerParams(vmem_limit_bytes=60 * 2**20),
+        )(*args, *flat, *self.last)
+        self.last = [out[n_out - 1]]
+        return out
+
+
+def shaped(*shape, dtype=BF):
+    return jax.ShapeDtypeStruct(shape, dtype)
+
+
+(V_QB, V_VB, V_OB, V_G1, V_B1, V_CQB, V_CVB, V_COB, V_G2, V_B2, V_FOB, V_G3, V_B3) = range(13)
+
+
+def near_kernel(spot_ref, x_ref, y_ref, vec_ref, wq_ref, wk_ref, wv_ref, uk_ref, uv_ref, q_ref, k_ref, v_ref, mk_ref, mv_ref):
+    x, y = x_ref[0], y_ref[0]
+    q_ref[...] = (dot(x, wq_ref[...]) + vec_ref[V_QB : V_QB + 1, :]).astype(BF)
+    k_ref[...] = dot(x, wk_ref[...]).astype(BF)
+    v_ref[...] = (dot(x, wv_ref[...]) + vec_ref[V_VB : V_VB + 1, :]).astype(BF)
+    mk_ref[...] = dot(y, uk_ref[...]).astype(BF)
+    mv_ref[...] = (dot(y, uv_ref[...]) + vec_ref[V_CVB : V_CVB + 1, :]).astype(BF)
+
+
+def project_near(order, spots, hidden_in, memory, vec, weights):
+    half, D = hidden_in.shape[1:]
+    x = pl.BlockSpec((1, half, D), lambda i, p: (p[4], 0, 0))
+    return order.call(
+        near_kernel, spots, hidden_in, memory, vec, *weights, scalars=1, name="project_near", us=8, grid=(1,),
+        in_specs=[x, x, full(vec.shape)] + [full((D, D))] * 5,
+        out_specs=[still((half, D))] * 5, out_shape=[shaped(half, D)] * 5)
+
+
+class Loads:
+    def __init__(self, sem):
+        self.sem = sem
+        self.copies = []
+
+    def add(self, src, dst):
+        self.copies.append(pltpu.make_async_copy(src, dst, self.sem.at[len(self.copies)]))
+        return self.copies[-1]
+
+
+def columns(p, width=128):
+    return pl.ds(pl.multiple_of(p * width, width), width)
+
+
+def self_kernel(spot_ref, vec_ref, oh_ref, mk_ref, hin_ref, hgot_ref, qn_ref, kn_ref, vn_ref, wq_ref, wk_ref, wv_ref, wo_ref, wc_ref,
+                l_ref, n_ref, r_ref, low_ref, cq_ref, h_out, q_out, k_out, v_out, m_out,
+                h_s, q_s, k_s, v_s, m_s, wq_s, wk_s, wv_s, wo_s, wc_s, sem, *, pairs, bq):
+    v = lambda i: vec_ref[i : i + 1, :]
+    at = pl.program_id(0)
+    half = hgot_ref.shape[0]
+    s = spot_ref[4]
+    near = pl.ds(pl.multiple_of(s * half, half), half)
+    far = pl.ds(pl.multiple_of((1 - s) * half, half), half)
+    loads = Loads(sem)
+    got = loads.add(hgot_ref, h_s.at[far])
+    in_q, in_k, in_v = loads.add(wq_ref, wq_s), loads.add(wk_ref, wk_s), loads.add(wv_ref, wv_s)
+    own = [loads.add(hin_ref.at[s], h_s.at[near])]
+    own += [loads.add(a, b.at[near]) for a, b in ((qn_ref, q_s), (kn_ref, k_s), (vn_ref, v_s))]
+    later = [loads.add(wo_ref, wo_s), loads.add(wc_ref, wc_s)]
+    outs = [loads.add(a, b) for a, b in ((h_s, h_out), (q_s, q_out), (k_s, k_out), (v_s, v_out))]
+    mixed_out = loads.add(m_s, m_out)
+
+    @pl.when(at == 0)
+    def _():
+        for c in (got, in_q, in_k, in_v, *own, *later):
+            c.start()
+        got.wait()
+        x = h_s[far, :]
+        in_q.wait()
+        q_s[far, :] = (dot(x, wq_s[...]) + v(V_QB)).astype(BF)
+        in_k.wait()
+        k_s[far, :] = dot(x, wk_s[...]).astype(BF)
+        in_v.wait()
+        v_s[far, :] = (dot(x, wv_s[...]) + v(V_VB)).astype(BF)
+        for c in own:
+            c.wait()
+        for c in outs:
+            c.start()
+
+    @pl.when((at > 0) & (at <= pairs))
+    def _():
+        cols = columns(at - 1)
+
+        def put_total(h, i, row):
+            l_ref[0, h : h + 1, i * bq : (i + 1) * bq] = row
+
+        blocks = attend_pair(q_s[:, cols], k_s[:, cols], v_s[:, cols], oh_ref[...], mk_ref[...], put_total, bq, True)
+        for i, b in enumerate(blocks):
+            m_s[i * bq : (i + 1) * bq, cols] = b
+
+    @pl.when(at == pairs + 1)
+    def _():
+        mixed_out.start()
+        for c in later:
+            c.wait()
+
+    @pl.when(at > pairs)
+    def _():
+        rows = pl.ds(pl.multiple_of((at - pairs - 1) * half, half), half)
+        x = h_s[rows, :].astype(F32) + (dot(m_s[rows, :], wo_s[...]) + v(V_OB))
+        n, r = norm_stats(x)
+        n_ref[...] = n
+        r_ref[...] = r
+        low = (n * v(V_G1) + v(V_B1)).astype(BF)
+        low_ref[...] = low
+        cq_ref[...] = (dot(low, wc_s[...]) + v(V_CQB)).astype(BF)
+
+    @pl.when(at == pairs + 2)
+    def _():
+        for c in (*outs, mixed_out):
+            c.wait()
+
+
+def self_forward(order, spots, vec, oh, mk, hidden_in, hidden_got, near, weights):
+    half, D = hidden_got.shape
+    T, pairs = 2 * half, D // 128
+    token = lambda width: pl.BlockSpec((half, width), lambda i, p: (jnp.maximum(i - pairs - 1, 0), 0))
+    hbm = pl.BlockSpec(memory_space=pl.ANY)
+    return order.call(
+        functools.partial(self_kernel, pairs=pairs, bq=512), spots, vec, oh, mk, hidden_in, hidden_got, *near, *weights,
+        scalars=1, name="self_forward", us=25, grid=(pairs + 3,),
+        in_specs=[full(a.shape) for a in (vec, oh, mk)] + [hbm] * 10,
+        out_specs=[pl.BlockSpec((1, 8, T), lambda i, p: (jnp.clip(i - 1, 0, pairs - 1), 0, 0)),
+                   token(D), token(1), token(D), token(D)] + [hbm] * 5,
+        out_shape=[shaped(pairs, 8, T, dtype=F32), shaped(T, D, dtype=F32), shaped(T, 1, dtype=F32), shaped(T, D), shaped(T, D)]
+        + [shaped(T, D)] * 5,
+        scratch_shapes=[pltpu.VMEM((T, D), BF)] * 5 + [pltpu.VMEM((D, D), BF)] * 5 + [pltpu.SemaphoreType.DMA((15,))])
+
+
+def cross_kernel(spot_ref, vec_ref, oh_ref, mask_ref, cq_ref, min_ref, mgot_ref, kn_ref, vn_ref, uk_ref, uv_ref,
+                 l_ref, m_out, k_out, v_out, c_out, m_s, k_s, v_s, q_s, c_s, uk_s, uv_s, sem, *, pairs, bq):
+    at = pl.program_id(0)
+    half = mgot_ref.shape[0]
+    s = spot_ref[4]
+    near = pl.ds(pl.multiple_of(s * half, half), half)
+    far = pl.ds(pl.multiple_of((1 - s) * half, half), half)
+    loads = Loads(sem)
+    got = loads.add(mgot_ref, m_s.at[far])
+    in_k, in_v = loads.add(uk_ref, uk_s), loads.add(uv_ref, uv_s)
+    own = [loads.add(min_ref.at[s], m_s.at[near]), loads.add(cq_ref, q_s)]
+    own += [loads.add(kn_ref, k_s.at[near]), loads.add(vn_ref, v_s.at[near])]
+    outs = [loads.add(a, b) for a, b in ((m_s, m_out), (k_s, k_out), (v_s, v_out))]
+
+    @pl.when(at == 0)
+    def _():
+        for c in (got, in_k, in_v, *own):
+            c.start()
+        got.wait()
+        x = m_s[far, :]
+        in_k.wait()
+        k_s[far, :] = dot(x, uk_s[...]).astype(BF)
+        in_v.wait()
+        v_s[far, :] = (dot(x, uv_s[...]) + vec_ref[V_CVB : V_CVB + 1, :]).astype(BF)
+        for c in own:
+            c.wait()
+        for c in outs:
+            c.start()
+
+    @pl.when(at > 0)
+    def _():
+        cols = columns(at - 1)
+
+        def put_total(h, i, row):
+            l_ref[0, h : h + 1, i * bq : (i + 1) * bq] = row
+
+        blocks = attend_pair(q_s[:, cols], k_s[:, cols], v_s[:, cols], oh_ref[...], mask_ref[...], put_total, bq, False)
+        for i, b in enumerate(blocks):
+            c_out[i * bq : (i + 1) * bq, :] = b
+
+    @pl.when(at == pairs)
+    def _():
+        for c in outs:
+            c.wait()
+
+
+def cross_forward(order, spots, vec, oh, mask, cq, memory, memory_got, near, weights):
+    half, D = memory_got.shape
+    T, pairs = 2 * half, D // 128
+    hbm = pl.BlockSpec(memory_space=pl.ANY)
+    pair = lambda i: jnp.maximum(i - 1, 0)
+    return order.call(
+        functools.partial(cross_kernel, pairs=pairs, bq=512), spots, vec, oh, mask, cq, memory, memory_got, *near, *weights,
+        scalars=1, name="cross_forward", us=23, grid=(pairs + 1,),
+        in_specs=[full(a.shape) for a in (vec, oh, mask)] + [hbm] * 7,
+        out_specs=[pl.BlockSpec((1, 8, T), lambda i, p: (pair(i), 0, 0))] + [hbm] * 3
+        + [pl.BlockSpec((T, 128), lambda i, p: (0, pair(i)))],
+        out_shape=[shaped(pairs, 8, T, dtype=F32)] + [shaped(T, D)] * 4,
+        scratch_shapes=[pltpu.VMEM((T, D), BF)] * 4 + [pltpu.VMEM((16, 128), BF)] + [pltpu.VMEM((D, D), BF)] * 2
+        + [pltpu.SemaphoreType.DMA((10,))])
+
+
+def ffn_kernel(spot_ref, vec_ref, bin_ref, n1_ref, cm_ref, og_ref, oggot_ref, wco_ref, win_ref, wout_ref,
+               own_ref, other_ref, sb_ref, cmb_ref, vo_ref, vi_ref, all_ref,
+               act_s, ib_s, cm_s, og_s, wco_s, win_s, wout_s, fb_s, low_s, cb_s, stage_s, stage_sem, sem, *, parts):
+    v = lambda i: vec_ref[i : i + 1, :]
+    t = pl.program_id(0)
+    half, D = oggot_ref.shape
+    s = spot_ref[4]
+    loads = Loads(sem)
+    in_cm, in_co = loads.add(cm_ref, cm_s), loads.add(wco_ref, wco_s)
+    in_up, in_down = loads.add(win_ref, win_s), loads.add(wout_ref, wout_s)
+    in_og = [loads.add(og_ref.at[s], og_s.at[s]), loads.add(oggot_ref, og_s.at[1 - s])]
+
+    def need(*copies):
+        @pl.when(t == 0)
+        def _():
+            for c in copies:
+                c.wait()
+
+    @pl.when(t == 0)
+    def _():
+        for c in loads.copies:
+            c.start()
+        vo_ref[...] = jnp.zeros_like(vo_ref)
+        vi_ref[...] = jnp.zeros_like(vi_ref)
+
+    @pl.when(t < 2)
+    def _():
+        need(in_cm, in_co)
+        rows = pl.ds(pl.multiple_of(t * half, half), half)
+        first = n1_ref[...] * v(V_G1) + v(V_B1)
+        n2, r2 = norm_stats(first + (dot(cm_s[rows, :], wco_s[...]) + v(V_COB)))
+        second = n2 * v(V_G2) + v(V_B2)
+        low = second.astype(BF)
+        low_s[rows, :] = low
+        need(in_up, in_down, *in_og)
+        width = win_s.shape[1] // parts
+        branch = None
+        for c in range(parts):
+            cols = slice(c * width, (c + 1) * width)
+            act, slope = gelu_pair(dot(low, win_s[:, cols]) + bin_ref[:, cols])
+            ib_s[rows, cols] = slope.astype(BF)
+            act = act.astype(BF)
+            act_s[rows, cols] = act
+            term = dot(act, wout_s[cols, :])
+            branch = term if branch is None else branch + term
+        n3, r3 = norm_stats(second + (branch + v(V_FOB)))
+        ho = (n3 * v(V_G3) + v(V_B3)).astype(BF)
+
+        @pl.when(t == s)
+        def _():
+            own_ref[...] = ho
+
+        @pl.when(t != s)
+        def _():
+            other_ref[...] = ho
+
+        e = og_s[t].astype(F32)
+        third = norm_back(e, n3, r3, v(V_G3))
+        fb = third.astype(BF)
+        fb_s[rows, :] = fb
+        vo_ref[0:1, :] += sums(e * n3)
+        vo_ref[1:2, :] += sums(e)
+        vo_ref[2:3, :] += sums(fb.astype(F32))
+        e = third
+        for c in range(parts):
+            cols = slice(c * width, (c + 1) * width)
+            ib = (nt(fb, wout_s[cols, :]) * ib_s[rows, cols].astype(F32)).astype(BF)
+            ib_s[rows, cols] = ib
+            vi_ref[:, cols] += sums(ib.astype(F32))
+            e = e + nt(ib, win_s[:, cols])
+        back = norm_back(e, n2, r2, v(V_G2))
+        sb_ref[...] = back
+        cb = back.astype(BF)
+        cb_s[rows, :] = cb
+        vo_ref[3:4, :] += sums(e * n2)
+        vo_ref[4:5, :] += sums(e)
+        vo_ref[5:6, :] += sums(cb.astype(F32))
+        cmb_ref[...] = nt(cb, wco_s[...]).astype(BF)
+
+    t = t - 2
+    slot = t % 2
+
+    def tall(b, slot):
+        return pltpu.make_async_copy(stage_s.at[slot], all_ref.at[b, :, pl.ds(0, 4)], stage_sem.at[slot])
+
+    def flat(b, slot):
+        return pltpu.make_async_copy(stage_s.at[slot], all_ref.at[:, :, 4 + b], stage_sem.at[slot])
+
+    @pl.when((t >= 2) & (t < 6))
+    def _():
+        tall(t - 2, slot).wait()
+
+    @pl.when(t >= 6)
+    def _():
+        flat(t - 6, slot).wait()
+
+    def put(x, g):
+        stage_s[slot] = tn(x, g).astype(BF).reshape(4, 4, 48, D)
+
+    @pl.when((t >= 0) & (t < 4))
+    def _():
+        put(act_s[:, columns(t, D)], fb_s[...])
+        tall(t, slot).start()
+
+    @pl.when((t >= 4) & (t < 8))
+    def _():
+        put(low_s[...], ib_s[:, columns(t - 4, D)])
+        flat(t - 4, slot).start()
+
+    @pl.when(t == 8)
+    def _():
+        put(cm_s[...], cb_s[...])
+        flat(4, 0).start()
+        flat(3, 1).wait()
+        flat(4, 0).wait()
+
+
+def ffn_both(order, spots, vec, bin_, n1, cm, out_grad, out_grad_got, weights):
+    half, D = out_grad_got.shape
+    T, FF = 2 * half, bin_.shape[1]
+    token = lambda width: pl.BlockSpec((half, width), lambda i, p: (jnp.minimum(i, 1), 0))
+    hbm = pl.BlockSpec(memory_space=pl.ANY)
+    big = lambda *shape: pltpu.VMEM(shape, BF)
+    return order.call(
+        functools.partial(ffn_kernel, parts=4), spots, vec, bin_, n1, cm, out_grad, out_grad_got, *weights,
+        scalars=1, name="ffn_both", us=60, grid=(11,),
+        in_specs=[full(vec.shape), full(bin_.shape), token(D)] + [hbm] * 6,
+        out_specs=[still((half, D)), still((half, D)), token(D), token(D), still((8, D)), still((1, FF)), hbm],
+        out_shape=[shaped(half, D), shaped(half, D), shaped(T, D, dtype=F32), shaped(T, D),
+                   shaped(8, D, dtype=F32), shaped(1, FF, dtype=F32), shaped(4, 4, 9, 48, D)],
+        scratch_shapes=[big(T, FF), big(T, FF), big(T, D), big(2, half, D), big(D, D), big(D, FF), big(FF, D), big(T, D), big(T, D),
+                        big(T, D), big(2, 4, 4, 48, D), pltpu.SemaphoreType.DMA((2,)), pltpu.SemaphoreType.DMA((6,))])
+
+
+def middle_kernel(spot_ref, vec_ref, q_ref, n_ref, r_ref, sb_ref,
+                  k_in, v_in, low_in, src_in, mix_in, wq_in, wk_in, wv_in, wo_in,
+                  fb_ref, mb_ref, own_ref, other_ref, vo_ref, send_ref, keep_ref,
+                  dq_s, dk_s, dv_s, back_s, low_s, src_s, mix_s, wq_s, wk_s, wv_s, wo_s, sem):
+    v = lambda i: vec_ref[i : i + 1, :]
+    t = pl.program_id(0)
+    half, D = own_ref.shape
+    loads = Loads(sem)
+    first = [loads.add(wq_in, wq_s), loads.add(wo_in, wo_s)]
+    more = [loads.add(a, b) for a, b in ((wk_in, wk_s), (wv_in, wv_s), (k_in, dk_s), (v_in, dv_s))]
+    last = [loads.add(a, b) for a, b in ((low_in, low_s), (src_in, src_s), (mix_in, mix_s))]
+
+    @pl.when(t == 0)
+    def _():
+        for c in loads.copies:
+            c.start()
+        vo_ref[...] = jnp.zeros_like(vo_ref)
+        for c in first:
+            c.wait()
+
+    @pl.when(t < 2)
+    def _():
+        rows = pl.ds(pl.multiple_of(t * half, half), half)
+        dq = q_ref[...]
+        dq_s[rows, :] = dq
+        n = n_ref[...]
+        e = sb_ref[...] + nt(dq, wq_s[...])
+        back = norm_back(e, n, r_ref[...], v(V_G1))
+        fb_ref[...] = back
+        low = back.astype(BF)
+        back_s[rows, :] = low
+        vo_ref[0:1, :] += sums(e * n)
+        vo_ref[1:2, :] += sums(e)
+        vo_ref[2:3, :] += sums(low.astype(F32))
+        vo_ref[3:4, :] += sums(dq.astype(F32))
+        mb_ref[...] = nt(low, wo_s[...]).astype(BF)
+
+        @pl.when(t == 0)
+        def _():
+            for c in more:
+                c.wait()
+
+        dv = dv_s[rows, :]
+        vo_ref[4:5, :] += sums(dv.astype(F32))
+        mg = (nt(dk_s[rows, :], wk_s[...]) + nt(dv, wv_s[...])).astype(BF)
+
+        @pl.when(t == spot_ref[4])
+        def _():
+            own_ref[...] = mg
+
+        @pl.when(t != spot_ref[4])
+        def _():
+            other_ref[...] = mg
+
+    @pl.when(t == 2)
+    def _():
+        for c in last:
+            c.wait()
+
+    for i, (x, g) in enumerate(((low_s, dq_s), (src_s, dk_s), (src_s, dv_s), (mix_s, back_s))):
+        @pl.when(t == 2 + i)
+        def _():
+            total = tn(x[...], g[...]).astype(BF)
+            def put_piece(which, x, zl, zh, rows):
+                for k in range(2):
+                    (send_ref, keep_ref)[which][at_of(ORDERS["cross"], x=x, y=k, zl=zl, zh=zh) + (0,)] = rows[:, D // 2 * k : D // 2 * (k + 1)]
+
+            place_rows(spot_ref[0], total, 48, put_piece)
+
+
+def middle(order, spots, vec, dq, dk, dv, n1, r1, sb, low, source, mixed, weights):
+    T, D = n1.shape
+    half = T // 2
+    token = lambda width: pl.BlockSpec((half, width), lambda i, p: (jnp.minimum(i, 1), 0))
+    out = pl.BlockSpec((2, 2, 2, 2, 1, 48, D // 2), lambda i, p: (0, 0, 0, 0, jnp.maximum(i - 2, 0), 0, 0))
+    hbm = pl.BlockSpec(memory_space=pl.ANY)
+    square, rect = pltpu.VMEM((D, D), BF), pltpu.VMEM((T, D), BF)
+    return order.call(
+        middle_kernel, spots, vec, dq, n1, r1, sb, dk, dv, low, source, mixed, *weights, scalars=1, name="middle", us=18,
+        grid=(6,),
+        in_specs=[full(vec.shape)] + [token(D), token(D), token(1), token(D)] + [hbm] * 9,
+        out_specs=[token(D), token(D), still((half, D)), still((half, D)), still((8, D)), out, out],
+        out_shape=[shaped(T, D, dtype=F32), shaped(T, D), shaped(half, D), shaped(half, D), shaped(8, D, dtype=F32)]
+        + [shaped(2, 2, 2, 2, 4, 48, D // 2)] * 2,
+        scratch_shapes=[rect] * 7 + [square] * 4 + [pltpu.SemaphoreType.DMA((9,))])
+
+
+def back_kernel(spot_ref, *refs, counts):
+    n = len(counts)
+    g, rest = refs[: sum(counts)], refs[sum(counts) :]
+    w, (plain_ref, own_ref, other_ref) = rest[:n], rest[n:]
+    total = plain_ref[...]
+    for i, count in enumerate(counts):
+        total = total + nt(joined(g[:count]), w[i][...])
+        g = g[count:]
+    total = total.astype(BF)
+
+    @pl.when(pl.program_id(0) == spot_ref[4])
+    def _():
+        own_ref[...] = total
+
+    @pl.when(pl.program_id(0) != spot_ref[4])
+    def _():
+        other_ref[...] = total
+
+
+def back_rows(order, spots, grads, weights, plain, moves):
+    parts = [p for g in grads for p in g]
+    T, D = plain.shape
+    half = T // 2
+    r = lambda width: pl.BlockSpec((half, width), lambda i, p: (i, 0))
+    return order.call(
+        functools.partial(back_kernel, counts=[len(g) for g in grads]), spots, *parts, *weights, plain,
+        scalars=1, name="back_rows", us=9, grid=(2,), moves=moves,
+        in_specs=[r(p.shape[1]) for p in parts] + [full((D, D))] * len(weights) + [r(D)],
+        out_specs=[still((half, D))] * 2, out_shape=[shaped(half, D)] * 2)
+
+
+def place_rows(core, total, height, put):
+    for j in range(total.shape[0] // (2 * height)):
+        even = total[2 * j * height : (2 * j + 1) * height]
+        odd = total[(2 * j + 1) * height : (2 * j + 2) * height]
+        put(1, j % 2, (j // 2) % 2, j // 4, jnp.where(core == 0, even, odd))
+        put(0, j % 2, (j // 2) % 2, j // 4, jnp.where(core == 0, odd, even))
+
+
+ORDERS = {"cross": ("y", "zl", "x", "zh"), "square": ("x", "zl", "zh")}
+
+
+def at_of(order, **place):
+    return tuple(place[name] for name in order)
+
+
+def joined(refs):
+    return refs[0][...] if len(refs) == 1 else jnp.concatenate([r[...] for r in refs], 1)
+
+
+def self_back_kernel(spot_ref, q_ref, k_ref, v_ref, do_ref, o_ref, l_ref, oh_ref, mk_ref, vf_ref, v1_ref, vi_ref, h_in,
+                     dq_ref, dk_ref, dv_ref, send_ref, keep_ref, keep_v_ref, acc_s, g_s, h_s, sem, *, pairs, bk):
+    at = pl.program_id(0)
+    hidden = pltpu.make_async_copy(h_in, h_s, sem)
+    D = 128 * pairs
+    wide = D // 2
+
+    @pl.when(at == 0)
+    def _():
+        hidden.start()
+
+    @pl.when(at < pairs)
+    def _():
+        out = {"q": (dq_ref, 0), "k": (dk_ref, 1), "v": (dv_ref, 2)}
+
+        def put(name, rows, block):
+            ref, i = out[name]
+            ref[rows, :] = block
+            g_s[i, rows, columns(at)] = block
+
+        attend_pair_back(q_ref[...], k_ref[...], v_ref[...], do_ref[...], o_ref[...], [l_ref[0, h : h + 1, :] for h in (0, 1)],
+                         oh_ref[...], mk_ref[...], acc_s, put, bk, True)
+
+    core = spot_ref[0]
+    tail = keep_ref.shape[0]
+
+    for i in range(3):
+        @pl.when(at == pairs + i)
+        def _():
+            if i == 0:
+                hidden.wait()
+
+            def put_piece(which, x, zl, zh, rows):
+                j = 4 * x + 2 * zl + zh
+                for k in range(2):
+                    part = rows[:, wide * k : wide * (k + 1)]
+                    if i < 2:
+                        at_row = 96 * (2 * j + i) + 48 * k
+                        (send_ref, keep_ref)[which][at_row : at_row + 48, :] = part
+                    elif which:
+                        keep_v_ref[128 * j + 64 * k : 128 * j + 64 * k + 48, :] = part
+                    else:
+                        send_ref[tail + 128 * j + 64 * k : tail + 128 * j + 64 * k + 48, :] = part
+
+            place_rows(core, tn(h_s[...], g_s[i]).astype(BF), 48, put_piece)
+
+    @pl.when(at == pairs + 2)
+    def _():
+        row_of = lambda i: sums(g_s[i].astype(F32))
+        rows = jnp.concatenate([vf_ref[0:6, :], v1_ref[0:5, :], row_of(0), row_of(2), jnp.zeros((3, D), F32)], 0)
+        spread = jnp.broadcast_to(vi_ref[...], (16, vi_ref.shape[1]))
+        for first, part, w in ((0, rows, 48), (128, spread, 192)):
+            for j in range(8):
+                x, zl, zh = j % 2, (j // 2) % 2, j // 4
+                even = part[:, 2 * j * w : (2 * j + 1) * w].astype(BF)
+                odd = part[:, (2 * j + 1) * w : (2 * j + 2) * w].astype(BF)
+                at_row = 128 * (4 * x + 2 * zl + zh) + 48
+                keep_v_ref[at_row : at_row + 16, first : first + w] = jnp.where(core == 0, even, odd)
+                send_ref[tail + at_row : tail + at_row + 16, first : first + w] = jnp.where(core == 0, odd, even)
+
+
+def self_back(order, spots, q, k, v, do, o, totals, oh, mk, vectors, hidden, moves):
+    T, D = q.shape
+    pairs = D // 128
+    p_in = lambda i: jnp.minimum(i, pairs - 1)
+    pair = pl.BlockSpec((T, 128), lambda i, p: (0, p_in(i)))
+    rows = 16 * 2 * 48, 16 * 64
+    return order.call(
+        functools.partial(self_back_kernel, pairs=pairs, bk=256), spots, q, k, v, do, o, totals, oh, mk, *vectors, hidden,
+        scalars=1, name="self_back", us=30, grid=(pairs + 3,), moves=moves,
+        in_specs=[pair] * 5 + [pl.BlockSpec((1, 8, T), lambda i, p: (p_in(i), 0, 0))]
+        + [full(a.shape) for a in (oh, mk, *vectors)] + [pl.BlockSpec(memory_space=pl.ANY)],
+        out_specs=[pair] * 3 + [still((r, D // 2)) for r in (sum(rows), *rows)],
+        out_shape=[shaped(T, D)] * 3 + [shaped(r, D // 2) for r in (sum(rows), *rows)],
+        scratch_shapes=[pltpu.VMEM((128, T), F32), pltpu.VMEM((3, T, D), BF), pltpu.VMEM((T, D), BF), pltpu.SemaphoreType.DMA])
+
+
+def fold_kernel(spot_ref, *refs, kinds):
+    n_in = sum(4 if k else 2 for k in kinds)
+    ins, outs = refs[:n_in], refs[n_in:]
+    for splits in kinds:
+        if splits:
+            keep, keep_other, got, got_other = ins[:4]
+            ins = ins[4:]
+            outs[0][...] = keep[0] + got[0]
+            outs[1][...] = keep_other[0] + got_other[0]
+            outs = outs[2:]
+        else:
+            outs[0][...] = ins[0][...] + ins[1][...]
+            ins, outs = ins[2:], outs[1:]
+
+
+def small_fold_kernel(spot_ref, *refs, items, keeps, gots):
+    keep_refs, got_refs, outs = refs[:keeps], refs[keeps : keeps + gots], refs[keeps + gots :]
+    for i, (g, at, which, message, first) in enumerate(items):
+        keep, got, out = keep_refs[i], got_refs[g], outs[i]
+        rows = out.shape[0]
+        if which is None:
+            total = keep[...] + got[at : at + rows, :]
+            out[...] = total
+        else:
+            mine = spot_ref[which]
+            part = lambda p: pl.ds(pl.multiple_of(p * rows, 16), rows)
+            there = lambda p: pl.ds(pl.multiple_of(at + p * rows, 16), rows)
+            out[...] = keep[part(mine), :] + got[there(mine), :]
+            total = keep[part(1 - mine), :] + got[there(1 - mine), :]
+        if message is not None:
+            outs[keeps + message][first : first + rows, :] = total
+
+
+LINKS = {"core": ("dp", 1, 16, 0), "x": ("dp", 2, 16, 1), "zl": ("dp", 4, 16, 2), "zh": ("dp", 8, 16, 3),
+         "y": ("seq", 1, 2, 4), "sum": ("seq", 1, 2, None), "gather": ("seq", 1, 2, None)}
+
+
+class Sum:
+    def __init__(self, keep, got, at, *links):
+        self.keep, self.got, self.at = keep, got, at
+        self.links, self.step = links, 0
+
+    def link(self):
+        return self.links[self.step] if self.step < len(self.links) else None
+
+
+def first_swap(send, keep, after=None):
+    if after is not None:
+        send, _ = lax.optimization_barrier((send, after))
+    flat = lambda a: a.reshape(-1, a.shape[-1])
+    return flat(keep), swap(flat(send), *LINKS["core"][:3])
+
+
+def advance(order, spots, *groups):
+    groups = [g for g in groups if g.link() is not None]
+    whichs = [LINKS[g.link()][3] for g in groups]
+    rows = [g.keep.shape[0] // (1 if w is None else 2) for g, w in zip(groups, whichs)]
+    shared = {}
+    for i, g in enumerate(groups):
+        shared.setdefault((LINKS[g.link()][:3], g.keep.shape[1]), []).append(i)
+    steps = next(s for s in (4, 2, 1) if all(r % (16 * s) == 0 for r in rows))
+    simple = all(len(s) == 1 for s in shared.values()) and all(g.got.shape == g.keep.shape for g in groups)
+    if simple and steps > 1:
+        args, in_specs, out_specs, out_shape = [], [], [], []
+        for g, w, r in zip(groups, whichs, rows):
+            width, bt = g.keep.shape[1], r // steps
+            flat = pl.BlockSpec((bt, width), lambda i, p: (i, 0))
+            if w is None:
+                args += [g.keep, g.got]
+                in_specs += [flat, flat]
+            else:
+                keep, got = g.keep.reshape(2, r, width), g.got.reshape(2, r, width)
+                mine = pl.BlockSpec((1, bt, width), lambda i, p, w=w: (p[w], i, 0))
+                other = pl.BlockSpec((1, bt, width), lambda i, p, w=w: (1 - p[w], i, 0))
+                args += [keep, keep, got, got]
+                in_specs += [mine, other, mine, other]
+            n = 1 if w is None else 2
+            out_specs += [flat] * n
+            out_shape += [shaped(r, width)] * n
+        out = list(order.call(
+            functools.partial(fold_kernel, kinds=[w is not None for w in whichs]), spots, *args, scalars=1, name="fold", us=3,
+            grid=(steps,), in_specs=in_specs, out_specs=out_specs, out_shape=out_shape))
+        for g, w in zip(groups, whichs):
+            g.keep = out.pop(0)
+            g.got, g.at = swap(g.keep if w is None else out.pop(0), *LINKS[g.link()][:3]), 0
+            g.step += 1
+        return
+    gots, items, messages = [], [], []
+    for g in groups:
+        if not any(a is g.got for a in gots):
+            gots.append(g.got)
+    place = {}
+    for key, members in shared.items():
+        if len(members) == 1 and whichs[members[0]] is None:
+            continue
+        first = 0
+        for i in members:
+            place[i] = (len(messages), first)
+            first += rows[i]
+        messages.append((first, key[1]))
+    for i, (g, w) in enumerate(zip(groups, whichs)):
+        items.append((next(n for n, a in enumerate(gots) if a is g.got), g.at, w, *place.get(i, (None, 0))))
+    shapes = [(r, g.keep.shape[1]) for r, g in zip(rows, groups)] + messages
+    arrays = [g.keep for g in groups] + gots
+    out = order.call(
+        functools.partial(small_fold_kernel, items=items, keeps=len(groups), gots=len(gots)), spots, *arrays, scalars=1,
+        name="fold", us=3, grid=(1,), in_specs=[full(a.shape) for a in arrays],
+        out_specs=[still(s) for s in shapes], out_shape=[shaped(*s) for s in shapes])
+    came = {}
+    for i, g in enumerate(groups):
+        g.keep = out[i]
+        links = LINKS[g.link()][:3]
+        if i not in place:
+            g.got, g.at = swap(g.keep, *links), 0
+        else:
+            message, first = place[i]
+            if message not in came:
+                came[message] = swap(out[len(groups) + message], *links)
+            g.got, g.at = came[message], first
+        g.step += 1
+
+
+def finish_kernel(spot_ref, *refs, items, keeps, gots):
+    ffn_ref, *refs = refs
+    keep_refs, got_refs, outs = refs[:keeps], refs[keeps : keeps + gots], list(refs[keeps + gots :])
+    values = []
+    for i, (g, at, join) in enumerate(items):
+        own = keep_refs[i][...]
+        got = got_refs[g][at : at + own.shape[0], :]
+        if join:
+            first = spot_ref[4] == 0
+            values.append((jnp.where(first, own, got), jnp.where(first, got, own)))
+        else:
+            values.append(own + got)
+    cross, self_qk, self_v = values
+    (sq, sk, sv, so, cq, ck, cv, co, fi, fo, *vectors) = outs
+    f32 = lambda v: v.astype(F32)
+    D = ffn_ref.shape[1]
+    w = D // 2
+    unit = lambda v, u: f32(v[48 * u : 48 * u + 48])
+    fo[...] = f32(ffn_ref[0:192, :])
+    for b in range(4):
+        fi[:, D * b : D * (b + 1)] = f32(ffn_ref[192 + 48 * b : 240 + 48 * b, :])
+    co[...] = f32(ffn_ref[384:432, :])
+    for k in range(2):
+        cols = slice(k * w, (k + 1) * w)
+        for i, o in enumerate((cq, ck, cv, so)):
+            o[:, cols] = unit(cross[k], i)
+        for i, o in enumerate((sq, sk)):
+            o[:, cols] = unit(self_qk, 2 * i + k)
+        sv[:, cols] = f32(self_v[64 * k : 64 * k + 48])
+    rows = f32(self_v[48:64])
+    for i, o in enumerate(vectors[:13]):
+        o[...] = rows[i : i + 1, :48]
+    vectors[13][...] = rows[0:1, 128:320]
+
+
+def finish(order, spots, ffn, *groups):
+    D = ffn.shape[1]
+    gots = []
+    for g in groups:
+        if not any(a is g.got for a in gots):
+            gots.append(g.got)
+    items = [(next(n for n, a in enumerate(gots) if a is g.got), g.at, g.links[-1] == "gather") for g in groups]
+    arrays = [ffn] + [g.keep for g in groups] + gots
+    shapes = [(48, D)] * 8 + [(48, 4 * D), (192, D)] + [(1, 48)] * 13 + [(1, 192)]
+    return order.call(
+        functools.partial(finish_kernel, items=items, keeps=len(groups), gots=len(gots)), spots, *arrays, scalars=1,
+        name="finish", us=3, grid=(1,), in_specs=[full(a.shape) for a in arrays], out_specs=[still(s) for s in shapes],
+        out_shape=[shaped(*s, dtype=F32) for s in shapes])
+
+
+def swap(block, ax, bit, size):
+    return lax.ppermute(block, ax, [(i, i ^ bit) for i in range(size)])
+
+
+def two(s, first, second):
+    return jnp.where(s == 0, jnp.concatenate([first, second], 0), jnp.concatenate([second, first], 0))
+
+
+def pick(array, index, axis):
+    return lax.dynamic_index_in_dim(array, index, axis, keepdims=False)
+
+
+def row_in(array, s):
+    own = pick(array, s, 0)
+    other = swap(pick(array, 1 - s, 0), "seq", 1, 2)
+    return two(s, own, other)
+
+
+def whole_rows(
+    hidden_in, memory, tgt_segment, src_segment, out_grad,
+    self_query, query_bias, self_key, self_value, value_bias, self_output, output_bias,
+    first_gain, first_shift,
+    cross_query, cross_query_bias, cross_key, cross_value, cross_value_bias, cross_output,
+    cross_output_bias, second_gain, second_shift,
+    ffn_in, ffn_in_bias, ffn_out, ffn_out_bias, third_gain, third_shift,
+):
+    f32 = lambda v: v.astype(F32)
+    s = lax.axis_index("seq")
+    dp = lax.axis_index("dp")
+    place = dp % 2, (dp // 2) % 2, (dp // 4) % 2, dp // 8, s
+    spots = jnp.stack(place).astype(jnp.int32)
+    order = Order()
+    far_half = lambda array: pick(array, 1 - s, 0)
+    segs = row_in(jnp.stack([tgt_segment, src_segment], -1), s)
+    hidden_got = swap(far_half(hidden_in), "seq", 1, 2)
+    vec = jnp.stack([query_bias, value_bias, output_bias, first_gain, first_shift, cross_query_bias, cross_value_bias,
+                     cross_output_bias, second_gain, second_shift, ffn_out_bias, third_gain, third_shift]).astype(F32)
+    bin_ = f32(ffn_in_bias).reshape(1, -1)
+    tgt, src = segs[:, 0], segs[:, 1]
+    self_oh, self_mk = masks(tgt, tgt)
+    _, cross_mk = masks(tgt, src)
+    *near_self, near_key, near_value = project_near(
+        order, spots, hidden_in, memory, vec, [self_query, self_key, self_value, cross_key, cross_value])
+    next_half, hidden_got, near_self[0] = lax.optimization_barrier((far_half(memory), hidden_got, near_self[0]))
+    memory_got = swap(next_half, "seq", 1, 2)
+    self_totals, n1, r1, first_low, cross_queries, hidden, queries, key_rows, value_rows, self_mixed = self_forward(
+        order, spots, vec, self_oh, self_mk, hidden_in, hidden_got, near_self,
+        [self_query, self_key, self_value, self_output, cross_query])
+    next_half, memory_got, r1 = lax.optimization_barrier((far_half(out_grad), memory_got, r1))
+    out_grad_got = swap(next_half, "seq", 1, 2)
+    cross_totals, source, memory_keys, memory_values, cross_mixed = cross_forward(
+        order, spots, vec, self_oh, cross_mk, cross_queries, memory, memory_got, [near_key, near_value], [cross_key, cross_value])
+    ho, ho_far, second_back, cross_mixed_back, v_ffn, v_in, ffn_all = ffn_both(
+        order, spots, vec, bin_, n1, cross_mixed, out_grad, out_grad_got, [cross_output, ffn_in, ffn_out])
+    ho_got = swap(ho_far, "seq", 1, 2)
+    ffn_sum = lax.psum(lax.psum_scatter(ffn_all.reshape(16, 432, -1), "dp", scatter_dimension=0, tiled=False), "seq")
+    cross_parts = attend_bwd(order, spots, cross_queries, memory_keys, memory_values, cross_mixed_back, cross_mixed, cross_totals,
+                             self_oh, cross_mk, False, 512)
+    order.last.append(ho_got)
+    first_back, self_mixed_back, mg, mg_far, v_first, *pairs = middle(
+        order, spots, vec, *cross_parts, n1, r1, second_back, first_low, source, self_mixed,
+        [cross_query, cross_key, cross_value, self_output])
+    cross_sum = Sum(*first_swap(*pairs), 0, *ORDERS["cross"], "gather")
+    advance(order, spots, cross_sum)
+    query_back, key_back, value_back, send, keep_qk, keep_v, hidden_out = self_back(
+        order, spots, queries, key_rows, value_rows, self_mixed_back, self_mixed, self_totals, self_oh, self_mk,
+        [v_ffn, v_first, v_in], hidden, [(ho, ho_got)])
+    advance(order, spots, cross_sum)
+    keep_qk, got = first_swap(send, keep_qk, cross_sum.keep)
+    qk_sum = Sum(keep_qk, got, 0, *ORDERS["square"], "sum")
+    v_sum = Sum(keep_v, got, keep_qk.shape[0], "sum", *ORDERS["square"])
+    advance(order, spots, qk_sum, v_sum)
+    hg, hg_far = back_rows(
+        order, spots, [[query_back], [key_back], [value_back]], [self_query, self_key, self_value], first_back, [])
+    mg_far, _ = lax.optimization_barrier((mg_far, keep_v))
+    mg_got = swap(mg_far, "seq", 1, 2)
+    hg_got = swap(hg_far, "seq", 1, 2)
+    for _ in range(3):
+        advance(order, spots, cross_sum, qk_sum, v_sum)
+    memory_grad = two(s, mg[None], mg_got[None])
+    hidden_grad = two(s, hg[None], hg_got[None])
+    (g_sq, g_sk, g_sv, g_so, g_cq, g_ck, g_cv, g_co, g_fi, g_fo, *v, v_fi) = finish(
+        order, spots, ffn_sum, cross_sum, qk_sum, v_sum)
+    (g3, b3, fob, g2, b2, cob, g1, b1, ob, cqb, cvb, qb, vb) = [a.reshape(-1) for a in v]
+    return (
+        hidden_out, hidden_grad, memory_grad,
+        g_sq, qb, g_sk, g_sv, vb, g_so, ob, g1, b1, g_cq, cqb, g_ck, g_cv, cvb, g_co, cob, g2, b2,
+        g_fi, v_fi.reshape(-1), g_fo, fob, g3, b3,
+    )
+
+
 def solution(mesh):
     in_specs = (
         P("dp", "seq", None),
@@ -443,6 +1473,13 @@
         P("dp"),
         P("dp"),
     )
+    rows_form = mesh.shape["seq"] == 2 and mesh.shape["dp"] == 16
+
+    def on_device(*arrays):
+        if rows_form and arrays[0].shape[0] == 2:
+            return whole_rows(*arrays)
+        return split_rows(*arrays)
+
     return jax.shard_map(
         on_device, mesh=mesh, in_specs=in_specs, out_specs=out_specs, check_vma=False
     )

time: 1540 us -> 365 us (0.24)
  matrix products: 673 us -> 0 us
  waiting for transfers between devices: 589 us -> 57 us
  Pallas kernels: 0 us -> 246 us
  other arithmetic: 113 us -> 5.85 us
  blocking collectives: 72.9 us -> 0 us
  local copies, waits for them, and re-layouts: 65.4 us -> 14.1 us
  starting transfers between devices: 1.25 us -> 23.6 us
    dot_general x42 -> x0, matrix products: 673 us -> none  [the longest x2 167 us: attend_backward(): jnp.einsum('rhqk,rqhd->rkhd', score_grads, split_heads(queries), preferre...]
    reduce_scatter x9 -> x1, waiting for transfers between devices: 338 us -> 0.01 us  [whole_rows(): lax.psum_scatter(ffn_all.reshape(16, 432, -1), 'dp', scatter_dimension=0,...]
    pallas_call x0 -> x15, Pallas kernels: none -> 246 us  [call(): pl.pallas_call(run, name=name, out_shape=list(out_shape) + [shaped(2, *pa...]
    unnamed x24 -> x2, waiting for transfers between devices: 227 us -> 0.03 us
    reduce_sum x13 -> x0, other arithmetic: 59.3 us -> none  [the longest x2 44.6 us: attend_forward(): totals = jnp.sum(powers, axis=-1, keepdims=True)]
    unnamed x1 -> x0, blocking collectives: 58.1 us -> none
    ppermute x0 -> x19, waiting for transfers between devices: none -> 57 us  [swap(): return lax.ppermute(block, ax, [(i, i ^ bit) for i in range(size)])]
    convert_element_type x36 -> x3, other arithmetic: 50.6 us -> 2.44 us  [the longest x1 1.13 us: masks(): jnp.where(c < 4, jnp.where(c == seg_k[:, None], 0.0, BIG), jnp.where(c <...]
  transfers between devices with their start and end apart: 19 -> 21, of which waited for: 11 -> 12; matrix products, arithmetic and copies ran while one was open for 44% -> 2% of each run, Pallas kernels for 0% -> 50%
where the time goes in v2:
time: 365 us; the launch traced here: 361 us
  Pallas kernels  246 us (67%)
  waiting for transfers between devices  57 us (16%)
  starting transfers between devices  23.6 us (6%)
  between operations  15 us (4%)
  local copies, waits for them, and re-layouts  14.1 us (4%)
  other arithmetic  5.85 us (2%)
    pallas_call x15, Pallas kernels, call(): pl.pallas_call(run, name=name, out_shape=list(out_shape) + [shaped(2, *pa...  246 us
    ppermute x19, waiting for transfers between devices, swap(): return lax.ppermute(block, ax, [(i, i ^ bit) for i in range(size)])  57 us
    ppermute x19, starting transfers between devices, swap(): return lax.ppermute(block, ax, [(i, i ^ bit) for i in range(size)])  23.5 us
    unnamed x82, local copies, waits for them, and re-layouts  10.1 us
  transfers between devices with their start and end apart: 21, of which 12 were waited for; matrix products, arithmetic and copies ran while one was open for 2% of the time, Pallas kernels for 50%

profile of v2, /device:TPU:0, one launch (start us, length us, event | category | flops | bytes accessed | tf_op | source)
XLA Modules:
  0.0 361.5 jit_solution(5780942067946716048)
XLA Ops:
  7.3 2.2 dynamic-slice_bitcast_fusion.1
  9.5 3.0 collective-permute-start.1
  15.6 8.0 %project_near.1 = (bf16[512,768]{1,0:T(8,128)(2,1)}, bf16[512,768]{1,0:T(8,128)(2,1)}, bf16[512,768]{1,0:T(8,128)(2,1)}, bf16[512,768]{1,0:T(8,128)(2,1)}, bf16[512,768]{1,0:T(8,128)(2,1)}) custom-call(s32[5]{0:T(128)} %stack.74.refs_0_, bf16[2,512,768]{2,1,0:T(8,128)(2,1)} %refs_4_.4, bf16[2,512,768]{2,1,0:T(8,128)(2,1)} %refs_5_.5, ...), custom_call_target="tpu_custom_call" | custom-call | bytes 57600000 | tf_op jit(solution)/shard_map/project_near/pallas_call | solution.py:606
  23.5 6.9 %collective-permute-done.1.refs_5_ = bf16[512,768]{1,0:T(8,128)(2,1)} collective-permute-done((bf16[512,768]{1,0:T(8,128)(2,1)}, bf16[512,768]{1,0:T(8,128)(2,1)}, u32[]{:S(2)}, u32[]{:S(2)}) %collective-permute-start.1) | collective-permute-done | bytes 786464 | tf_op jit(solution)/shard_map/ppermute | solution.py:1325
  30.4 1.7 collective-permute-start.2
  34.0 25.7 %self_forward.1 = (f32[6,8,1024]{2,1,0:T(8,128)}, f32[1024,768]{1,0:T(8,128)}, f32[1024,1]{1,0:T(8,128)}, bf16[1024,768]{1,0:T(8,128)(2,1)}, bf16[1024,768]{1,0:...) custom-call(s32[5]{0:T(128)} %stack.74.refs_0_, ...), custom_call_target="tpu_custom_call" | custom-call | bytes 180000000 | tf_op jit(solution)/shard_map/self_forward/pallas_call | solution.py:606
  60.7 23.9 %cross_forward.1 = (f32[6,8,1024]{2,1,0:T(8,128)}, bf16[1024,768]{1,0:T(8,128)(2,1)}, bf16[1024,768]{1,0:T(8,128)(2,1)}, bf16[1024,768]{1,0:T(8,128)(2,1)}, bf16[1024,768]{1,0:T(8,128)(2,1)}) custom-call(s32[5]{0:T(128)} %stack.74.refs_0_, f32[13,768]{1,0:T(8,128)} %convert_element_type.13.refs_3_.refs_1_, bf16[64,1024]{1,0:T(8,128)(2,1)} %fusion.refs_2_.refs_7_, ...), custom_call_target="tpu_custom_call" | custom-call | bytes 165600000 | tf_op jit(solution)/shard_map/cross_forward/pallas_call | solution.py:606
  85.5 62.3 %ffn_both.1 = (bf16[512,768]{1,0:T(8,128)(2,1)}, bf16[512,768]{1,0:T(8,128)(2,1)}, f32[1024,768]{1,0:T(8,128)}, bf16[1024,768]{1,0:T(8,128)(2,1)}, f32[8,768]{1,...) custom-call(s32[5]{0:T(128)} %stack.74.refs_0_, f32[13,768]{1,0:T(8,128)} %convert_element_type.13.refs_3_.refs_1_, ...), custom_call_target="tpu_custom_call" | custom-call | bytes 432000000 | tf_op jit(solution)/shard_map/ffn_both/pallas_call | solution.py:606
  149.0 1.7 collective-permute-start.4
  150.7 35.1 %attend_bwd.1 = (bf16[1024,768]{1,0:T(8,128)(2,1)}, bf16[1024,768]{1,0:T(8,128)(2,1)}, bf16[1024,768]{1,0:T(8,128)(2,1)}) custom-call(s32[5]{0:T(128)} %stack.74.refs_0_, bf16[1024,768]{1,0:T(8,128)(2,1)} %get-tuple-element.136.refs_4_.refs_1_, bf16[1024,768]{1,0:T(8,128)(2,1)} %get-tuple-element.142.refs_2_, bf16[1024,768]{1,0:T(8,128)(2,1)} %get-tuple-element.143.refs_3_, ...), custom_call_target="tpu_custom_call" | custom-call | bytes 172800000 | tf_op jit(solution)/shard_map/attend_bwd/pallas_call | solution.py:606
  186.8 22.4 %middle.1 = (f32[1024,768]{1,0:T(8,128)}, bf16[1024,768]{1,0:T(8,128)(2,1)}, bf16[512,768]{1,0:T(8,128)(2,1)}, bf16[512,768]{1,0:T(8,128)(2,1)}, f32[8,768]{1,0:...) custom-call(s32[5]{0:T(128)} %stack.74.refs_0_, ...), custom_call_target="tpu_custom_call" | custom-call | bytes 129600000 | tf_op jit(solution)/shard_map/middle/pallas_call | solution.py:606
  209.2 4.7 %collective-permute-done.5 = bf16[3072,384]{1,0:T(8,128)(2,1)S(1)} collective-permute-done((bf16[3072,384]{1,0:T(8,128)(2,1)}, bf16[3072,384]{1,0:T(8,128)(2,1)S(1)}, u32[]{:S(2)}, u32[]{:S(2)}) %collective-permute-start.5) | collective-permute-done | bytes 2359328 | tf_op jit(solution)/shard_map/ppermute | solution.py:1325
  215.5 5.0 %fold.6 = (bf16[1536,384]{1,0:T(8,128)(2,1)}, bf16[1536,384]{1,0:T(8,128)(2,1)}) custom-call(s32[5]{0:T(128)} %stack.74.refs_0_, bf16[2,1536,384]{2,1,0:T(8,128)(2,1)} %bitcast.48, bf16[2,1536,384]{2,1,0:T(8,128)(2,1)} %bitcast.49, bf16[2,1536,384]{2,1,0:T(8,128)(2,1)} %bitcast.50, bf16[2,1536,384]{2,1,0:T(8,128)(2,1)} %bitcast.51, ...), custom_call_target="tpu_custom_call" | custom-call | bytes 21600000 | tf_op jit(solution)/shard_map/fold/pallas_call | solution.py:606
  220.8 30.9 %self_back.1 = (bf16[1024,768]{1,0:T(8,128)(2,1)}, bf16[1024,768]{1,0:T(8,128)(2,1)}, bf16[1024,768]{1,0:T(8,128)(2,1)}, bf16[2560,384]{1,0:T(8,128)(2,1)}, bf16...) custom-call(s32[5]{0:T(128)} %stack.74.refs_0_, ...), custom_call_target="tpu_custom_call" | custom-call | bytes 216000000 | tf_op jit(solution)/shard_map/self_back/pallas_call | solution.py:606
  252.8 4.4 %fold.7 = (bf16[768,384]{1,0:T(8,128)(2,1)}, bf16[768,384]{1,0:T(8,128)(2,1)}) custom-call(s32[5]{0:T(128)} %stack.74.refs_0_, bf16[2,768,384]{2,1,0:T(8,128)(2,1)} %bitcast.52, bf16[2,768,384]{2,1,0:T(8,128)(2,1)} %bitcast.53, bf16[2,768,384]{2,1,0:T(8,128)(2,1)} %bitcast.54, bf16[2,768,384]{2,1,0:T(8,128)(2,1)} %bitcast.55, ...), custom_call_target="tpu_custom_call" | custom-call | bytes 21600000 | tf_op jit(solution)/shard_map/fold/pallas_call | solution.py:606
  257.2 4.2 %collective-permute-done.7.refs_3_ = bf16[2560,384]{1,0:T(8,128)(2,1)S(1)} collective-permute-done((bf16[2560,384]{1,0:T(8,128)(2,1)}, bf16[2560,384]{1,0:T(8,128)(2,1)S(1)}, u32[]{:S(2)}, u32[]{:S(2)}) %collective-permute-start.7) | collective-permute-done | bytes 1966112 | tf_op jit(solution)/shard_map/ppermute | solution.py:1325
  262.8 4.5 %fold.8 = (bf16[768,384]{1,0:T(8,128)(2,1)}, bf16[1024,384]{1,0:T(8,128)(2,1)}, bf16[768,384]{1,0:T(8,128)(2,1)}) custom-call(s32[5]{0:T(128)} %stack.74.refs_0_, bf16[1536,384]{1,0:T(8,128)(2,1)} %get-tuple-element.173.refs_1_, bf16[1024,384]{1,0:T(8,128)(2,1)} %get-tuple-element.174.refs_5_.refs_2_, bf16[2560,384]{1,0:T(8,128)(2,1)} %copy-done.5, ...), custom_call_target="tpu_custom_call" | custom-call | bytes 21600000 | tf_op jit(solution)/shard_map/fold/pallas_call | solution.py:606
  267.3 1.7 collective-permute-start.12
  272.0 9.6 %back_rows.1 = (bf16[512,768]{1,0:T(8,128)(2,1)}, bf16[512,768]{1,0:T(8,128)(2,1)}) custom-call(s32[5]{0:T(128)} %stack.74.refs_0_, bf16[1024,768]{1,0:T(8,128)(2,1)} %get-tuple-element.169.refs_1_, bf16[1024,768]{1,0:T(8,128)(2,1)} %get-tuple-element.170.refs_2_, bf16[1024,768]{1,0:T(8,128)(2,1)} %get-tuple-element.171.refs_3_, bf16[768,768]{1,0:T(8,128)(2,1)} %refs_4_.5, ...), custom_call_target="tpu_custom_call" | custom-call | bytes 64800000 | tf_op jit(solution)/shard_map/back_rows/pallas_call | solution.py:606
  281.6 2.5 collective-permute-done.10.refs_4_
  288.0 4.4 %fold.9 = (bf16[384,384]{1,0:T(8,128)(2,1)}, bf16[384,384]{1,0:T(8,128)(2,1)}, bf16[512,384]{1,0:T(8,128)(2,1)}, bf16[896,384]{1,0:T(8,128)(2,1)}, bf16[384,384]{1,0:T(8,128)(2,1)}) custom-call(s32[5]{0:T(128)} %stack.74.refs_0_, bf16[768,384]{1,0:T(8,128)(2,1)} %get-tuple-element.177.refs_1_, bf16[768,384]{1,0:T(8,128)(2,1)} %get-tuple-element.186.refs_2_, ...), custom_call_target="tpu_custom_call" | custom-call | bytes 21600000 | tf_op jit(solution)/shard_map/fold/pallas_call | solution.py:606
  292.4 1.7 collective-permute-start.13
  297.8 5.9 %collective-permute-done.14.refs_5_ = bf16[384,384]{1,0:T(8,128)(2,1)S(1)} collective-permute-done((bf16[384,384]{1,0:T(8,128)(2,1)}, bf16[384,384]{1,0:T(8,128)(2,1)S(1)}, u32[]{:S(2)}, u32[]{:S(2)}) %collective-permute-start.14) | collective-permute-done | bytes 294944 | tf_op jit(solution)/shard_map/ppermute | solution.py:1325
  303.7 5.5 %collective-permute-done.13.refs_4_ = bf16[896,384]{1,0:T(8,128)(2,1)S(1)} collective-permute-done((bf16[896,384]{1,0:T(8,128)(2,1)}, bf16[896,384]{1,0:T(8,128)(2,1)S(1)}, u32[]{:S(2)}, u32[]{:S(2)}) %collective-permute-start.13) | collective-permute-done | bytes 688160 | tf_op jit(solution)/shard_map/ppermute | solution.py:1325
  310.1 3.3 fold.10
  313.4 3.0 collective-permute-start.15
  317.9 8.0 %collective-permute-done.16.refs_5_ = bf16[256,384]{1,0:T(8,128)(2,1)S(1)} collective-permute-done((bf16[256,384]{1,0:T(8,128)(2,1)}, bf16[256,384]{1,0:T(8,128)(2,1)S(1)}, u32[]{:S(2)}, u32[]{:S(2)}) %collective-permute-start.16) | collective-permute-done | bytes 196640 | tf_op jit(solution)/shard_map/ppermute | solution.py:1325
  325.9 2.7 collective-permute-done.15.refs_4_
  329.3 2.8 fold.11
  335.1 10.8 %collective-permute-done.8 = bf16[512,768]{1,0:T(8,128)(2,1)S(1)} collective-permute-done((bf16[512,768]{1,0:T(8,128)(2,1)S(1)}, bf16[512,768]{1,0:T(8,128)(2,1)S(1)}, u32[]{:S(2)}, u32[]{:S(2)}) %collective-permute-start.8) | collective-permute-done | bytes 786464 | tf_op jit(solution)/shard_map/ppermute | solution.py:1325
  347.3 2.9 collective-permute-done.17.refs_5_
  350.9 3.5 finish.1
  (139 shorter events, 31.5 us)
Async XLA Ops:
  7.2 5.3 %copy-start.25 = (s32[2,512]{1,0:T(2,128)S(1)}, s32[2,512]{1,0:T(2,128)}, u32[]{:S(2)}) copy-start(s32[2,512]{1,0:T(2,128)} %param.32) | copy-start | bytes 12292
  7.2 5.3 %copy-start.24 = (s32[2,512]{1,0:T(2,128)S(1)}, s32[2,512]{1,0:T(2,128)}, u32[]{:S(2)}) copy-start(s32[2,512]{1,0:T(2,128)} %param.31) | copy-start | bytes 12292
  7.2 5.5 %copy-start.3 = (bf16[2,512,768]{2,1,0:T(8,128)(2,1)S(1)}, bf16[2,512,768]{2,1,0:T(8,128)(2,1)}, u32[]{:S(2)}) copy-start(bf16[2,512,768]{2,1,0:T(8,128)(2,1)} %refs_5_.6) | copy-start | bytes 4718596
  7.2 290.6 %reduce-scatter.2.cloned.1.call-start = ((), (), s32[]{:S(2)}) async-start(), calls=%async_computation.1 | async-start | bytes 11280384 | tf_op jit(solution)/shard_map/reduce_scatter | solution.py:1379
  7.3 6.5 %copy-start = (bf16[2,512,768]{2,1,0:T(8,128)(2,1)S(1)}, bf16[2,512,768]{2,1,0:T(8,128)(2,1)}, u32[]{:S(2)}) copy-start(bf16[2,512,768]{2,1,0:T(8,128)(2,1)} %refs_5_.5) | copy-start | bytes 4718596
  9.5 20.9 %collective-permute-start.1 = (bf16[512,768]{1,0:T(8,128)(2,1)}, bf16[512,768]{1,0:T(8,128)(2,1)}, u32[]{:S(2)}, u32[]{:S(2)}) collective-permute-start(bf16[512,768]{1,0:T(8,128)(2,1)} %dynamic-slice_bitcast_fusion.1), channel_id=1, source_target_pairs={{0,1},{1,0},{2,3},{3,2},{4,5},{5,4},{6,7},{7,6},{8,9},{9,8},{10,11... | collective-permute-start | bytes 2359304 | tf_op jit(solution)/shard_map/ppermute | solution.py:1325
  12.5 19.6 %collective-permute-start = (s32[512,2]{0,1:T(2,128)S(1)}, s32[512,2]{0,1:T(2,128)S(1)}, u32[]{:S(2)}, u32[]{:S(2)}) collective-permute-start(s32[512,2]{0,1:T(2,128)S(1)} %bitcast.68), channel_id=1, source_target_pairs={{0,1},{1,0},{2,3},{3,2},{4,5},{5,4},{6,7},{7,6},{8,9},{9,8},{10,11... | collective-permute-start | bytes 12296 | tf_op jit(solution)/shard_map/ppermute | solution.py:1325
  30.4 29.3 %collective-permute-start.2 = (bf16[512,768]{1,0:T(8,128)(2,1)S(1)}, bf16[512,768]{1,0:T(8,128)(2,1)S(1)}, u32[]{:S(2)}, u32[]{:S(2)}) collective-permute-start(bf16[512,768]{1,0:T(8,128)(2,1)S(1)} %dynamic-slice_bitcast_fusion.2), channel_id=1, source_target_pairs={{0,1},{1,0},{2,3},{3,2},{4,5},{5,4},{6,7},{7,6},{8,9},{9,8},{10,11... | collective-permute-start | bytes 2359304 | tf_op jit(solution)/shard_map/ppermute | solution.py:1325
  34.0 25.8 %copy-start.10 = (bf16[512,768]{1,0:T(8,128)(2,1)S(1)}, bf16[512,768]{1,0:T(8,128)(2,1)}, u32[]{:S(2)}) copy-start(bf16[512,768]{1,0:T(8,128)(2,1)} %dynamic-slice_bitcast_fusion) | copy-start | bytes 2359300
  34.0 26.1 %copy-start.23 = (bf16[3072]{0:T(1024)(128)(2,1)S(1)}, bf16[3072]{0:T(1024)(128)(2,1)}, u32[]{:S(2)}) copy-start(bf16[3072]{0:T(1024)(128)(2,1)} %param.53) | copy-start | bytes 18436
  59.7 24.9 %collective-permute-start.3 = (bf16[512,768]{1,0:T(8,128)(2,1)S(1)}, bf16[512,768]{1,0:T(8,128)(2,1)S(1)}, u32[]{:S(2)}, u32[]{:S(2)}) collective-permute-start(bf16[512,768]{1,0:T(8,128)(2,1)S(1)} %copy-done.10), channel_id=1, source_target_pairs={{0,1},{1,0},{2,3},{3,2},{4,5},{5,4},{6,7},{7,6},{8,9},{9,8},{10,11... | collective-permute-start | bytes 2359304 | tf_op jit(solution)/shard_map/ppermute | solution.py:1325
  147.9 202.2 %all-reduce.2.cloned.1.call-start = ((), (), s32[]{:S(2)}) async-start(), calls=%async_computation.2 | async-start | bytes 1327104 | tf_op jit(solution)/shard_map/psum | solution.py:1379
  149.0 36.9 %collective-permute-start.4 = (bf16[512,768]{1,0:T(8,128)(2,1)S(1)}, bf16[512,768]{1,0:T(8,128)(2,1)S(1)}, u32[]{:S(2)}, u32[]{:S(2)}) collective-permute-start(bf16[512,768]{1,0:T(8,128)(2,1)S(1)} %copy-done.39), channel_id=1, source_target_pairs={{0,1},{1,0},{2,3},{3,2},{4,5},{5,4},{6,7},{7,6},{8,9},{9,8},{10,11... | collective-permute-start | bytes 2359304 | tf_op jit(solution)/shard_map/ppermute | solution.py:1325
  209.2 4.8 %collective-permute-start.5 = (bf16[3072,384]{1,0:T(8,128)(2,1)}, bf16[3072,384]{1,0:T(8,128)(2,1)S(1)}, u32[]{:S(2)}, u32[]{:S(2)}) collective-permute-start(bf16[3072,384]{1,0:T(8,128)(2,1)} %bitcast.69), channel_id=1, source_target_pairs={{0,2},{2,0},{4,6},{6,4},{8,10},{10,8},{12,14},{14,12},{16,18},{18,... | collective-permute-start | bytes 7077896 | tf_op jit(solution)/shard_map/ppermute | solution.py:1325
  220.5 31.3 %collective-permute-start.6 = (bf16[1536,384]{1,0:T(8,128)(2,1)}, bf16[1536,384]{1,0:T(8,128)(2,1)S(1)}, u32[]{:S(2)}, u32[]{:S(2)}) collective-permute-start(bf16[1536,384]{1,0:T(8,128)(2,1)} %get-tuple-element.167.refs_15_), channel_id=1, source_target_pairs={{0,1},{1,0},{2,3},{3,2},{4,5},{5,4},{6,7},{7,6},{8,9},{9,8},{10,11... | collective-permute-start | bytes 3538952 | tf_op jit(solution)/shard_map/ppermute | solution.py:1325
  257.2 4.2 %collective-permute-start.7 = (bf16[2560,384]{1,0:T(8,128)(2,1)}, bf16[2560,384]{1,0:T(8,128)(2,1)S(1)}, u32[]{:S(2)}, u32[]{:S(2)}) collective-permute-start(bf16[2560,384]{1,0:T(8,128)(2,1)} %get-tuple-element.178), channel_id=1, source_target_pairs={{0,2},{2,0},{4,6},{6,4},{8,10},{10,8},{12,14},{14,12},{16,18},{18,... | collective-permute-start | bytes 5898248 | tf_op jit(solution)/shard_map/ppermute | solution.py:1325
  262.8 6.2 %copy-start.14 = (bf16[768,384]{1,0:T(8,128)(2,1)S(1)}, bf16[768,384]{1,0:T(8,128)(2,1)}, u32[]{:S(2)}) copy-start(bf16[768,384]{1,0:T(8,128)(2,1)} %get-tuple-element.179.refs_4_) | copy-start | bytes 1769476
  267.3 19.8 %collective-permute-start.12 = (bf16[1024,384]{1,0:T(8,128)(2,1)}, bf16[1024,384]{1,0:T(8,128)(2,1)S(1)}, u32[]{:S(2)}, u32[]{:S(2)}) collective-permute-start(bf16[1024,384]{1,0:T(8,128)(2,1)} %get-tuple-element.187.refs_3_), channel_id=1, source_target_pairs={{0,1},{1,0},{2,3},{3,2},{4,5},{5,4},{6,7},{7,6},{8,9},{9,8},{10,11... | collective-permute-start | bytes 2359304 | tf_op jit(solution)/shard_map/ppermute | solution.py:1325
  269.0 15.1 %collective-permute-start.10 = (bf16[768,384]{1,0:T(8,128)(2,1)S(1)}, bf16[768,384]{1,0:T(8,128)(2,1)S(1)}, u32[]{:S(2)}, u32[]{:S(2)}) collective-permute-start(bf16[768,384]{1,0:T(8,128)(2,1)S(1)} %copy-done.14), channel_id=1, source_target_pairs={{0,8},{2,10},{4,12},{6,14},{8,0},{10,2},{12,4},{14,6},{16,24},{18,... | collective-permute-start | bytes 1769480 | tf_op jit(solution)/shard_map/ppermute | solution.py:1325
  270.6 15.0 %collective-permute-start.11 = (bf16[768,384]{1,0:T(8,128)(2,1)}, bf16[768,384]{1,0:T(8,128)(2,1)S(1)}, u32[]{:S(2)}, u32[]{:S(2)}) collective-permute-start(bf16[768,384]{1,0:T(8,128)(2,1)} %get-tuple-element.180.refs_8_), channel_id=1, source_target_pairs={{0,4},{2,6},{4,0},{6,2},{8,12},{10,14},{12,8},{14,10},{16,20},{18,... | collective-permute-start | bytes 1769480 | tf_op jit(solution)/shard_map/ppermute | solution.py:1325
  287.9 7.6 %copy-start.7 = (bf16[512,768]{1,0:T(8,128)(2,1)S(1)}, bf16[512,768]{1,0:T(8,128)(2,1)}, u32[]{:S(2)}) copy-start(bf16[512,768]{1,0:T(8,128)(2,1)} %get-tuple-element.182.refs_7_) | copy-start | bytes 2359300
  292.4 16.8 %collective-permute-start.13 = (bf16[896,384]{1,0:T(8,128)(2,1)}, bf16[896,384]{1,0:T(8,128)(2,1)S(1)}, u32[]{:S(2)}, u32[]{:S(2)}) collective-permute-start(bf16[896,384]{1,0:T(8,128)(2,1)} %get-tuple-element.191), channel_id=1, source_target_pairs={{0,4},{2,6},{4,0},{6,2},{8,12},{10,14},{12,8},{14,10},{16,20},{18,... | collective-permute-start | bytes 2064392 | tf_op jit(solution)/shard_map/ppermute | solution.py:1325
  294.1 39.6 %collective-permute-start.9 = (bf16[512,768]{1,0:T(8,128)(2,1)}, bf16[512,768]{1,0:T(8,128)(2,1)S(1)}, u32[]{:S(2)}, u32[]{:S(2)}) collective-permute-start(bf16[512,768]{1,0:T(8,128)(2,1)} %get-tuple-element.185), channel_id=1, source_target_pairs={{0,1},{1,0},{2,3},{3,2},{4,5},{5,4},{6,7},{7,6},{8,9},{9,8},{10,11... | collective-permute-start | bytes 2359304 | tf_op jit(solution)/shard_map/ppermute | solution.py:1325
  295.6 50.3 %collective-permute-start.8 = (bf16[512,768]{1,0:T(8,128)(2,1)S(1)}, bf16[512,768]{1,0:T(8,128)(2,1)S(1)}, u32[]{:S(2)}, u32[]{:S(2)}) collective-permute-start(bf16[512,768]{1,0:T(8,128)(2,1)S(1)} %copy-done.7), channel_id=1, source_target_pairs={{0,1},{1,0},{2,3},{3,2},{4,5},{5,4},{6,7},{7,6},{8,9},{9,8},{10,11... | collective-permute-start | bytes 2359304 | tf_op jit(solution)/shard_map/ppermute | solution.py:1325
  296.1 7.6 %collective-permute-start.14 = (bf16[384,384]{1,0:T(8,128)(2,1)}, bf16[384,384]{1,0:T(8,128)(2,1)S(1)}, u32[]{:S(2)}, u32[]{:S(2)}) collective-permute-start(bf16[384,384]{1,0:T(8,128)(2,1)} %get-tuple-element.192.refs_6_), channel_id=1, source_target_pairs={{0,8},{2,10},{4,12},{6,14},{8,0},{10,2},{12,4},{14,6},{16,24},{18,... | collective-permute-start | bytes 884744 | tf_op jit(solution)/shard_map/ppermute | solution.py:1325
  303.7 6.4 %copy-start.17 = (bf16[384,384]{1,0:T(8,128)(2,1)}, bf16[384,384]{1,0:T(8,128)(2,1)S(1)}, u32[]{:S(2)}) copy-start(bf16[384,384]{1,0:T(8,128)(2,1)S(1)} %collective-permute-done.14.refs_5_) | copy-start | bytes 884740
  310.1 23.6 %copy-start.11 = (bf16[512,768]{1,0:T(8,128)(2,1)S(1)}, bf16[512,768]{1,0:T(8,128)(2,1)}, u32[]{:S(2)}) copy-start(bf16[512,768]{1,0:T(8,128)(2,1)} %get-tuple-element.183) | copy-start | bytes 2359300
  313.4 15.2 %collective-permute-start.15 = (bf16[384,384]{1,0:T(8,128)(2,1)}, bf16[384,384]{1,0:T(8,128)(2,1)S(1)}, u32[]{:S(2)}, u32[]{:S(2)}) collective-permute-start(bf16[384,384]{1,0:T(8,128)(2,1)} %get-tuple-element.196), channel_id=1, source_target_pairs={{0,16},{2,18},{4,20},{6,22},{8,24},{10,26},{12,28},{14,30},{16,0},... | collective-permute-start | bytes 884744 | tf_op jit(solution)/shard_map/ppermute | solution.py:1325
  316.4 9.5 %collective-permute-start.16 = (bf16[256,384]{1,0:T(8,128)(2,1)}, bf16[256,384]{1,0:T(8,128)(2,1)S(1)}, u32[]{:S(2)}, u32[]{:S(2)}) collective-permute-start(bf16[256,384]{1,0:T(8,128)(2,1)} %get-tuple-element.197.refs_6_), channel_id=1, source_target_pairs={{0,8},{2,10},{4,12},{6,14},{8,0},{10,2},{12,4},{14,6},{16,24},{18,... | collective-permute-start | bytes 589832 | tf_op jit(solution)/shard_map/ppermute | solution.py:1325
  332.1 18.1 %collective-permute-start.17 = (bf16[384,384]{1,0:T(8,128)(2,1)}, bf16[384,384]{1,0:T(8,128)(2,1)S(1)}, u32[]{:S(2)}, u32[]{:S(2)}) collective-permute-start(bf16[384,384]{1,0:T(8,128)(2,1)} %get-tuple-element.201), channel_id=1, source_target_pairs={{0,1},{1,0},{2,3},{3,2},{4,5},{5,4},{6,7},{7,6},{8,9},{9,8},{10,11... | collective-permute-start | bytes 884744 | tf_op jit(solution)/shard_map/ppermute | solution.py:1325
  333.7 12.2 %copy-start.12 = (bf16[512,768]{1,0:T(8,128)(2,1)S(1)}, bf16[512,768]{1,0:T(8,128)(2,1)}, u32[]{:S(2)}) copy-start(bf16[512,768]{1,0:T(8,128)(2,1)} %get-tuple-element.181) | copy-start | bytes 2359300
  335.1 12.2 %collective-permute-start.18 = (bf16[128,384]{1,0:T(8,128)(2,1)S(1)}, bf16[128,384]{1,0:T(8,128)(2,1)S(1)}, u32[]{:S(2)}, u32[]{:S(2)}) collective-permute-start(bf16[128,384]{1,0:T(8,128)(2,1)S(1)} %copy-done.21), channel_id=1, source_target_pairs={{0,16},{2,18},{4,20},{6,22},{8,24},{10,26},{12,28},{14,30},{16,0},... | collective-permute-start | bytes 294920 | tf_op jit(solution)/shard_map/ppermute | solution.py:1325
  (29 other events, 39.3 us)
Sparse Core Ops, SparseCore 0:
  148.0 121.6 reduce-scatter.1
  297.9 45.3 all-reduce.1
